TPU v7x, 256 devices: a whole 4x4x8 slice. The times are simulated.
256 devices in a mesh: face: 4 (over x), tile: 16 (over z, core), dp: 4 (over y).
Axes of the slice: x: 4, y: 4, z: 8, core: 2. Of those that a mesh axis runs over, the one named last changes fastest.
Arguments:
- inputs: bfloat16 [4, 384, 90, 2880], P('dp', ('face', 'tile')), may hold values from -6 to 6
- cotangent: bfloat16 [4, 384, 90, 2880], P('dp', ('face', 'tile')), may hold values from -6 to 6
- conv_weight: bfloat16 [288, 32], replicated, may hold values from -0.375 to 0.375
- out_bias: float32 [32], replicated, may hold values from -3 to 3
- cell_area: float32 [384, 8100], P(('face', 'tile')), may hold values from 0.25 to 4
- land_mask: int32 [384, 8100], P(('face', 'tile')), may hold values 0 or 1
- neighbours: int32 [384, 4], P(('face', 'tile')), may hold values from -1 to 383, as said below
- reversal: int32 [384, 4], P(('face', 'tile')), may hold values from 0 to 1, as said below
- wet_count: int32 [64], P(('face', 'tile')), may hold values from 1 to 6, as said below
Outputs:
- outputs: bfloat16 [4, 384, 90, 2880], P('dp', ('face', 'tile'))
- input_grad: bfloat16 [4, 384, 90, 2880], P('dp', ('face', 'tile'))
- weight_grad: float32 [288, 32], replicated
- bias_grad: float32 [32], replicated
Inputs may be any that keep to these rules, and one draw needn't show every extreme that they name: Device group g = face index * 16 + tile index holds slots g * 6 to g * 6 + 5. Entry [s, 0] is -1 or a slot of the group one step up along tile (wrapping), [s, 1] one step down along tile, [s, 2] one step up along face (wrapping), [s, 3] one step down along face. No entry names a slot at or past its group's wet_count, and a slot past its own group's wet_count has only -1. If neighbours[s, d] = m >= 0 then neighbours[m, (1, 0, 3, 2)[d]] = s. `reversal`: zero where neighbours is -1; equal on the two sides of each seam. `wet_count`: wet tiles of a group fill its slots from position 0; some group holds 6.
All inputs are finite; a program needn't handle non-finite values. No bound on the sum of `land_mask` on one device may be relied on, other than what follows from the above.
Results may differ from a plain program's by a relative error of at most 0.0049.
Values may be sent and summed in bfloat16 or wider, within the bound.
A program may use at most 192 MiB of HBM per device.

v0:
```python
import math

import jax
import jax.numpy as jnp
from jax import lax
from jax.sharding import PartitionSpec as P


def passed_along(block, axis, distance):
    devices = range(lax.axis_size(axis))
    route = [((i - distance) % len(devices), i) for i in devices]
    return lax.ppermute(block, axis, route)


def seam_route(pieces, neighbours, reversal, tile_len, channels):
    batch_rows, slot_total, length = pieces[0].shape
    sources = [
        passed_along(pieces[1], "tile", -1),
        passed_along(pieces[0], "tile", 1),
        passed_along(pieces[3], "face", -1),
        passed_along(pieces[2], "face", 1),
    ]
    local_slot = jnp.maximum(neighbours, 0) % slot_total
    arrived = [
        jnp.take(sources[side_index], local_slot[:, side_index], axis=1) for side_index in range(4)
    ]
    results = []
    for side_index in range(4):
        shaped = arrived[side_index].reshape(batch_rows, slot_total, tile_len, channels)
        flipped = shaped[:, :, ::-1]
        chosen = jnp.where((reversal[:, side_index] == 1)[None, :, None, None], flipped, shaped)
        results.append(
            jnp.where(
                (neighbours[:, side_index] >= 0)[None, :, None, None],
                chosen,
                jnp.zeros_like(chosen),
            )
        )
    return results


def unfold(padded_tile, tile_len, channels):
    parts = []
    for row_off in range(3):
        for col_off in range(3):
            parts.append(padded_tile[:, row_off : row_off + tile_len, col_off : col_off + tile_len])
    return jnp.concatenate(parts, -1).reshape(-1, 9 * channels)


def per_device(
    inputs, cotangent, conv_weight, out_bias, cell_area, land_mask, neighbours, reversal, wet_count
):
    batch_rows, slot_total, tile_len, wide_row = inputs.shape
    channels = wide_row // tile_len
    wet_total = wet_count[0]
    occupied = (jnp.arange(slot_total, dtype=jnp.int32) < wet_total).astype(jnp.float32)
    wet_cells = (
        land_mask.reshape(slot_total, tile_len, tile_len).astype(jnp.float32)
        * occupied[:, None, None]
    )
    tiles_in = inputs.reshape(batch_rows, slot_total, tile_len, tile_len, channels)
    masked = (tiles_in.astype(jnp.float32) * wet_cells[None, :, :, :, None]).astype(jnp.bfloat16)
    edges = [
        masked[:, :, 0],
        masked[:, :, tile_len - 1],
        masked[:, :, :, tile_len - 1],
        masked[:, :, :, 0],
    ]
    strips = seam_route(
        [edge.reshape(batch_rows, slot_total, -1) for edge in edges],
        neighbours,
        reversal,
        tile_len,
        channels,
    )
    corner = jnp.zeros((batch_rows, slot_total, 1, channels), jnp.bfloat16)
    top_row = jnp.concatenate([corner, strips[0], corner], 2)
    bottom_row = jnp.concatenate([corner, strips[1], corner], 2)
    middle = jnp.concatenate([strips[3][:, :, :, None], masked, strips[2][:, :, :, None]], 3)
    padded = jnp.concatenate([top_row[:, :, None], middle, bottom_row[:, :, None]], 2)
    area_cells = cell_area.reshape(slot_total, tile_len, tile_len)
    scaled = (
        wet_cells[None, :, :, :, None]
        * area_cells[None, :, :, :, None]
        * cotangent.reshape(batch_rows, slot_total, tile_len, tile_len, channels).astype(
            jnp.float32
        )
    ).astype(jnp.bfloat16)

    def step(slot_index, state_now):
        out_buffer, interior_buffer, rim_buffer, weight_acc, bias_acc = state_now
        tile_block = lax.dynamic_index_in_dim(padded, slot_index, 1, keepdims=False)
        grad_tile = lax.dynamic_index_in_dim(scaled, slot_index, 1, keepdims=False)
        wet_tile = lax.dynamic_index_in_dim(wet_cells, slot_index, 0, keepdims=False)
        patches = unfold(tile_block, tile_len, channels)
        result = jnp.dot(patches, conv_weight, preferred_element_type=jnp.float32) + out_bias
        produced = (
            wet_tile[None, :, :, None] * result.reshape(batch_rows, tile_len, tile_len, channels)
        ).astype(jnp.bfloat16)
        flat_grad = grad_tile.reshape(-1, channels)
        weight_acc = weight_acc + lax.dot_general(
            patches, flat_grad, (((0,), (0,)), ((), ())), preferred_element_type=jnp.float32
        )
        bias_acc = bias_acc + jnp.sum(flat_grad.astype(jnp.float32), 0)
        patch_grad = lax.dot_general(
            flat_grad, conv_weight, (((1,), (1,)), ((), ())), preferred_element_type=jnp.float32
        )
        pad_grad = jnp.zeros((batch_rows, tile_len + 2, tile_len + 2, channels), jnp.float32)
        for row_off in range(3):
            for col_off in range(3):
                start = (3 * row_off + col_off) * channels
                piece = patch_grad[:, start : start + channels].reshape(
                    batch_rows, tile_len, tile_len, channels
                )
                pad_grad = pad_grad + jnp.pad(
                    piece, ((0, 0), (row_off, 2 - row_off), (col_off, 2 - col_off), (0, 0))
                )
        rims = jnp.stack(
            [
                pad_grad[:, 0, 1:-1],
                pad_grad[:, tile_len + 1, 1:-1],
                pad_grad[:, 1:-1, tile_len + 1],
                pad_grad[:, 1:-1, 0],
            ],
            0,
        ).astype(jnp.bfloat16)
        out_buffer = lax.dynamic_update_index_in_dim(out_buffer, produced, slot_index, 1)
        interior_buffer = lax.dynamic_update_index_in_dim(
            interior_buffer, pad_grad[:, 1:-1, 1:-1], slot_index, 1
        )
        rim_buffer = lax.dynamic_update_index_in_dim(rim_buffer, rims, slot_index, 2)
        return (out_buffer, interior_buffer, rim_buffer, weight_acc, bias_acc)

    initial = (
        jnp.zeros((batch_rows, slot_total, tile_len, tile_len, channels), jnp.bfloat16),
        jnp.zeros((batch_rows, slot_total, tile_len, tile_len, channels), jnp.float32),
        jnp.zeros((4, batch_rows, slot_total, tile_len, channels), jnp.bfloat16),
        jnp.zeros((9 * channels, channels), jnp.float32),
        jnp.zeros((channels,), jnp.float32),
    )
    out_buffer, interior_buffer, rim_buffer, weight_acc, bias_acc = lax.fori_loop(
        0, wet_total, step, initial
    )
    weight_total, bias_total = lax.psum((weight_acc, bias_acc), ("face", "tile", "dp"))
    cell_norm = math.sqrt(
        batch_rows
        * lax.axis_size("dp")
        * slot_total
        * lax.axis_size("face")
        * lax.axis_size("tile")
        * tile_len
        * tile_len
    )
    weight_grad = weight_total / cell_norm
    bias_grad = bias_total / cell_norm
    returned = seam_route(
        [rim_buffer[side_index].reshape(batch_rows, slot_total, -1) for side_index in range(4)],
        neighbours,
        reversal,
        tile_len,
        channels,
    )
    last = tile_len - 1
    summed = interior_buffer
    summed = summed + jnp.pad(
        returned[0].astype(jnp.float32)[:, :, None], ((0, 0), (0, 0), (0, last), (0, 0), (0, 0))
    )
    summed = summed + jnp.pad(
        returned[1].astype(jnp.float32)[:, :, None], ((0, 0), (0, 0), (last, 0), (0, 0), (0, 0))
    )
    summed = summed + jnp.pad(
        returned[2].astype(jnp.float32)[:, :, :, None], ((0, 0), (0, 0), (0, 0), (last, 0), (0, 0))
    )
    summed = summed + jnp.pad(
        returned[3].astype(jnp.float32)[:, :, :, None], ((0, 0), (0, 0), (0, 0), (0, last), (0, 0))
    )
    input_grad = (
        (wet_cells[None, :, :, :, None] * summed).astype(jnp.bfloat16).reshape(inputs.shape)
    )
    outputs = out_buffer.reshape(inputs.shape)
    return (outputs, input_grad, weight_grad, bias_grad)


def solution(mesh):
    return jax.shard_map(
        per_device,
        mesh=mesh,
        in_specs=(
            P("dp", ("face", "tile"), None, None),
            P("dp", ("face", "tile"), None, None),
            P(),
            P(),
            P(("face", "tile"), None),
            P(("face", "tile"), None),
            P(("face", "tile"), None),
            P(("face", "tile"), None),
            P(("face", "tile")),
        ),
        out_specs=(
            P("dp", ("face", "tile"), None, None),
            P("dp", ("face", "tile"), None, None),
            P(),
            P(),
        ),
        check_vma=False,
    )
```

profile of v0, /device:TPU:1, one launch (start us, length us, event | category | flops | bytes accessed | tf_op | source)
XLA Modules:
  0.0 861.4 jit_solution(11541638721117150754)
XLA Ops:
  4.3 6.3 copy.136
  20.5 9.3 %slice_reduce_fusion.3 = (bf16[6,90,32]{2,1,0:T(8,128)(2,1)S(1)}, bf16[6,90,32]{2,1,0:T(8,128)(2,1)S(1)}) fusion(bf16[1,6,90,90,32]{2,4,3,1,0:T(8,128)(2,1)} %copy-done), kind=kLoop, calls=%fused_computation.40 | loop fusion | bytes 138240 | tf_op jit(solution)/shard_map/slice | solution.py:65
  33.8 6.3 copy.153
  40.1 5.4 fusion
  51.1 8.0 copy.150
  59.2 7.9 copy.151
  67.3 10.2 %pad_maximum_fusion = bf16[1,6,92,92,32]{2,4,3,1,0:T(8,128)(2,1)} fusion(bf16[1,6,1,92,32]{2,4,3,1,0:T(8,128)(2,1)} %copy.151, bf16[1,6,90,1,32]{2,4,3,1,0:T(8,128)(2,1)S(1)} %select_bitcast_fusion.4, bf16[1,6,90,90,32]{2,4,3,1,0:T(8,128)(2,1)} %copy-done, bf16[1,6,90,1,32]{2,4,3,1,0:T(8,128)(2,1)S(1)} %select_bitcast_fusion.5, ...), kind=kLoop, calls=%fused_computation.38 | loop fusion | flops 16250880 | bytes 6500352 | tf_op jit(solution)/shard_map/concatenate | solution.py:80
  84.9 338.2 %while.20 = (s32[]{:T(128)}, bf16[1,6,90,90,32]{2,4,3,1,0:T(8,128)(2,1)}, f32[1,6,90,90,32]{2,4,1,3,0:T(8,128)}, bf16[4,1,6,90,32]{3,4,2,1,0:T(8,128)(2,1)S(1)},...) while((s32[]{:T(128)}, ...), condition=%wide.region_2.4_spmd, body=%wide.region_0.3_spmd.sunk | while | flops 451732608 | bytes 109467120 | solution.py:141
  120.4 12.4 %reshape.549 = bf16[8100,288]{0,1:T(8,128)(2,1)} reshape(bf16[1,90,90,288]{2,1,3,0:T(8,128)(2,1)} %slice_dynamic-update-slice_fusion.26) | data formatting | bytes 9331200 | tf_op jit(solution)/shard_map/while/body/reshape | solution.py:47
  166.8 4.9 reshape.555
  171.7 4.9 reshape.556
  176.6 5.0 reshape.557
  181.6 4.9 reshape.558
  195.2 7.1 fusion.35
  222.9 12.4 %reshape.549 = bf16[8100,288]{0,1:T(8,128)(2,1)} reshape(bf16[1,90,90,288]{2,1,3,0:T(8,128)(2,1)} %slice_dynamic-update-slice_fusion.26) | data formatting | bytes 9331200 | tf_op jit(solution)/shard_map/while/body/reshape | solution.py:47
  269.3 4.9 reshape.555
  274.2 4.9 reshape.556
  279.1 5.0 reshape.557
  284.1 4.9 reshape.558
  297.7 7.1 fusion.35
  325.3 12.4 %reshape.549 = bf16[8100,288]{0,1:T(8,128)(2,1)} reshape(bf16[1,90,90,288]{2,1,3,0:T(8,128)(2,1)} %slice_dynamic-update-slice_fusion.26) | data formatting | bytes 9331200 | tf_op jit(solution)/shard_map/while/body/reshape | solution.py:47
  371.8 4.9 reshape.555
  376.7 4.9 reshape.556
  381.7 5.0 reshape.557
  386.6 4.9 reshape.558
  400.2 7.1 fusion.35
  423.0 385.5 %all-reduce.13 = (f32[288,32]{0,1:T(8,128)S(1)}, f32[32]{0:T(128)S(1)}) all-reduce(f32[288,32]{0,1:T(8,128)S(1)} %get-tuple-element.164, f32[32]{0:T(128)S(1)} %get-tuple-element.165), channel_id=1, replica_groups=mesh['face'=4,'tile'=16,'dp'=4] {'face','tile','dp'}, use_global_device_ids=true, to_apply=%region_3.5 | all-reduce | flops 9248 | bytes 73984 | tf_op jit(solution)/shard_map/psum | solution.py:144
  813.3 6.4 copy.173
  828.1 8.1 copy.160
  836.2 8.1 copy.165
  844.3 7.6 multiply_convert_fusion.1
  854.9 6.4 copy.174
  (284 shorter events, 232.9 us)
Async XLA Ops:
  16.3 30.2 %collective-permute-start.1 = (bf16[1,6,2880]{2,1,0:T(8,128)(2,1)S(1)}, bf16[1,6,2880]{2,1,0:T(8,128)(2,1)S(1)}, u32[]{:S(2)}, u32[]{:S(2)}) collective-permute-start(bf16[1,6,2880]{2,1,0:T(8,128)(2,1)S(1)} %reshape_squeeze.25), channel_id=1, source_target_pairs={{192,0},{0,64},{64,128},{128,192},{193,1},{1,65},{65,129},{129,193... | collective-permute-start | bytes 103688 | tf_op jit(solution)/shard_map/ppermute | solution.py:12
  18.8 14.6 %copy-start.4 = (s32[6,4]{0,1:T(4,128)S(1)}, s32[6,4]{0,1:T(4,128)}, u32[]{:S(2)}) copy-start(s32[6,4]{0,1:T(4,128)} %param.19) | copy-start | bytes 292
  18.8 14.7 %copy-start.33 = (s32[6,4]{0,1:T(4,128)S(1)}, s32[6,4]{0,1:T(4,128)}, u32[]{:S(2)}) copy-start(s32[6,4]{0,1:T(4,128)} %param.20) | copy-start | bytes 292
  18.8 28.4 %collective-permute-start.2 = (bf16[1,6,2880]{2,1,0:T(8,128)(2,1)S(1)}, bf16[1,6,2880]{2,1,0:T(8,128)(2,1)S(1)}, u32[]{:S(2)}, u32[]{:S(2)}) collective-permute-start(bf16[1,6,2880]{2,1,0:T(8,128)(2,1)S(1)} %reshape_squeeze.26), channel_id=1, source_target_pairs={{64,0},{128,64},{192,128},{0,192},{65,1},{129,65},{193,129},{1,193... | collective-permute-start | bytes 103688 | tf_op jit(solution)/shard_map/ppermute | solution.py:12
  30.0 19.6 %collective-permute-start.3 = (bf16[1,6,2880]{2,1,0:T(8,128)(2,1)S(1)}, bf16[1,6,2880]{2,1,0:T(8,128)(2,1)S(1)}, u32[]{:S(2)}, u32[]{:S(2)}) collective-permute-start(bf16[1,6,2880]{2,1,0:T(8,128)(2,1)S(1)} %reshape_squeeze.27), channel_id=1, source_target_pairs={{60,0},{0,4},{4,8},{8,12},{12,16},{16,20},{20,24},{24,28},{28,32},... | collective-permute-start | bytes 103688 | tf_op jit(solution)/shard_map/ppermute | solution.py:12
  33.2 14.7 %collective-permute-start = (bf16[1,6,2880]{2,1,0:T(8,128)(2,1)S(1)}, bf16[1,6,2880]{2,1,0:T(8,128)(2,1)S(1)}, u32[]{:S(2)}, u32[]{:S(2)}) collective-permute-start(bf16[1,6,2880]{2,1,0:T(8,128)(2,1)S(1)} %reshape_squeeze.24), channel_id=1, source_target_pairs={{4,0},{8,4},{12,8},{16,12},{20,16},{24,20},{28,24},{32,28},{36,32}... | collective-permute-start | bytes 103688 | tf_op jit(solution)/shard_map/ppermute | solution.py:12
  33.4 17.3 %copy-start.17 = (pred[6]{0:T(512)(128)(4,1)}, pred[6]{0:T(512)(128)(4,1)S(1)}, u32[]{:S(2)}) copy-start(pred[6]{0:T(512)(128)(4,1)S(1)} %get-tuple-element.289) | copy-start | bytes 22
  33.4 17.4 %copy-start.19 = (pred[6]{0:T(512)(128)(4,1)}, pred[6]{0:T(512)(128)(4,1)S(1)}, u32[]{:S(2)}) copy-start(pred[6]{0:T(512)(128)(4,1)S(1)} %get-tuple-element.291) | copy-start | bytes 22
  33.5 33.6 %copy-start.27 = (pred[6]{0:T(512)(128)(4,1)}, pred[6]{0:T(512)(128)(4,1)S(1)}, u32[]{:S(2)}) copy-start(pred[6]{0:T(512)(128)(4,1)S(1)} %get-tuple-element.290) | copy-start | bytes 22
  33.5 33.7 %copy-start.25 = (pred[6]{0:T(512)(128)(4,1)}, pred[6]{0:T(512)(128)(4,1)S(1)}, u32[]{:S(2)}) copy-start(pred[6]{0:T(512)(128)(4,1)S(1)} %get-tuple-element.292) | copy-start | bytes 22
  33.5 13.6 %copy-start.15 = (pred[6]{0:T(512)(128)(4,1)}, pred[6]{0:T(512)(128)(4,1)S(1)}, u32[]{:S(2)}) copy-start(pred[6]{0:T(512)(128)(4,1)S(1)} %get-tuple-element.301) | copy-start | bytes 22
  33.5 14.2 %copy-start.13 = (pred[6]{0:T(512)(128)(4,1)}, pred[6]{0:T(512)(128)(4,1)S(1)}, u32[]{:S(2)}) copy-start(pred[6]{0:T(512)(128)(4,1)S(1)} %get-tuple-element.299) | copy-start | bytes 22
  33.5 14.9 %copy-start.9 = (pred[6]{0:T(512)(128)(4,1)}, pred[6]{0:T(512)(128)(4,1)S(1)}, u32[]{:S(2)}) copy-start(pred[6]{0:T(512)(128)(4,1)S(1)} %get-tuple-element.260) | copy-start | bytes 22
  33.5 16.7 %copy-start.11 = (pred[6]{0:T(512)(128)(4,1)}, pred[6]{0:T(512)(128)(4,1)S(1)}, u32[]{:S(2)}) copy-start(pred[6]{0:T(512)(128)(4,1)S(1)} %get-tuple-element.297) | copy-start | bytes 22
  33.6 17.2 %copy-start.21 = (pred[6]{0:T(512)(128)(4,1)}, pred[6]{0:T(512)(128)(4,1)S(1)}, u32[]{:S(2)}) copy-start(pred[6]{0:T(512)(128)(4,1)S(1)} %get-tuple-element.293) | copy-start | bytes 22
  33.6 17.3 %copy-start.23 = (pred[6]{0:T(512)(128)(4,1)}, pred[6]{0:T(512)(128)(4,1)S(1)}, u32[]{:S(2)}) copy-start(pred[6]{0:T(512)(128)(4,1)S(1)} %get-tuple-element.295) | copy-start | bytes 22
  33.6 33.5 %copy-start.31 = (pred[6]{0:T(512)(128)(4,1)}, pred[6]{0:T(512)(128)(4,1)S(1)}, u32[]{:S(2)}) copy-start(pred[6]{0:T(512)(128)(4,1)S(1)} %get-tuple-element.294) | copy-start | bytes 22
  33.6 33.6 %copy-start.29 = (pred[6]{0:T(512)(128)(4,1)}, pred[6]{0:T(512)(128)(4,1)S(1)}, u32[]{:S(2)}) copy-start(pred[6]{0:T(512)(128)(4,1)S(1)} %get-tuple-element.296) | copy-start | bytes 22
  33.6 14.2 %copy-start.6 = (s32[1024]{0:T(1024)}, s32[1024]{0:T(1024)S(1)}, u32[]{:S(2)}) copy-start(s32[1024]{0:T(1024)S(1)} %pad_clamp_fusion.3) | copy-start | bytes 12292
  33.6 16.0 %copy-start.5 = (s32[1024]{0:T(1024)}, s32[1024]{0:T(1024)S(1)}, u32[]{:S(2)}) copy-start(s32[1024]{0:T(1024)S(1)} %pad_clamp_fusion) | copy-start | bytes 12292
  33.7 13.5 %copy-start.7 = (s32[1024]{0:T(1024)}, s32[1024]{0:T(1024)S(1)}, u32[]{:S(2)}) copy-start(s32[1024]{0:T(1024)S(1)} %pad_clamp_fusion.1) | copy-start | bytes 12292
  809.5 13.5 %collective-permute-start.7 = (bf16[1,6,2880]{2,1,0:T(8,128)(2,1)S(1)}, bf16[1,6,2880]{2,1,0:T(8,128)(2,1)S(1)}, u32[]{:S(2)}, u32[]{:S(2)}) collective-permute-start(bf16[1,6,2880]{2,1,0:T(8,128)(2,1)S(1)} %reshape_squeeze.31), channel_id=1, source_target_pairs={{192,0},{0,64},{64,128},{128,192},{193,1},{1,65},{65,129},{129,193... | collective-permute-start | bytes 103688 | tf_op jit(solution)/shard_map/ppermute | solution.py:12
  810.1 13.7 %collective-permute-start.6 = (bf16[1,6,2880]{2,1,0:T(8,128)(2,1)S(1)}, bf16[1,6,2880]{2,1,0:T(8,128)(2,1)S(1)}, u32[]{:S(2)}, u32[]{:S(2)}) collective-permute-start(bf16[1,6,2880]{2,1,0:T(8,128)(2,1)S(1)} %reshape_squeeze.30), channel_id=1, source_target_pairs={{64,0},{128,64},{192,128},{0,192},{65,1},{129,65},{193,129},{1,193... | collective-permute-start | bytes 103688 | tf_op jit(solution)/shard_map/ppermute | solution.py:12
  813.2 12.2 %copy-start.26 = (pred[6]{0:T(512)(128)(4,1)S(1)}, pred[6]{0:T(512)(128)(4,1)}, u32[]{:S(2)}) copy-start(pred[6]{0:T(512)(128)(4,1)} %copy-done.25) | copy-start | bytes 22
  813.2 12.2 %copy-start.30 = (pred[6]{0:T(512)(128)(4,1)S(1)}, pred[6]{0:T(512)(128)(4,1)}, u32[]{:S(2)}) copy-start(pred[6]{0:T(512)(128)(4,1)} %copy-done.29) | copy-start | bytes 22
  813.2 13.8 %copy-start.10 = (pred[6]{0:T(512)(128)(4,1)S(1)}, pred[6]{0:T(512)(128)(4,1)}, u32[]{:S(2)}) copy-start(pred[6]{0:T(512)(128)(4,1)} %copy-done.9) | copy-start | bytes 22
  813.2 13.8 %copy-start.12 = (pred[6]{0:T(512)(128)(4,1)S(1)}, pred[6]{0:T(512)(128)(4,1)}, u32[]{:S(2)}) copy-start(pred[6]{0:T(512)(128)(4,1)} %copy-done.11) | copy-start | bytes 22
  813.2 14.2 %copy-start.20 = (pred[6]{0:T(512)(128)(4,1)S(1)}, pred[6]{0:T(512)(128)(4,1)}, u32[]{:S(2)}) copy-start(pred[6]{0:T(512)(128)(4,1)} %copy-done.19) | copy-start | bytes 22
  813.3 14.2 %copy-start.24 = (pred[6]{0:T(512)(128)(4,1)S(1)}, pred[6]{0:T(512)(128)(4,1)}, u32[]{:S(2)}) copy-start(pred[6]{0:T(512)(128)(4,1)} %copy-done.23) | copy-start | bytes 22
  820.0 5.6 collective-permute-start.4
  821.6 4.7 collective-permute-start.5
  828.0 16.3 %copy-start.2 = (f32[6,90,90]{1,0,2:T(8,128)S(1)}, f32[6,90,90]{1,0,2:T(8,128)}, u32[]{:S(2)}) copy-start(f32[6,90,90]{1,0,2:T(8,128)} %copy.137) | copy-start | bytes 583204
  (10 other events, 75.6 us)
where the time goes:
time: 870 us; the launch traced here: 861 us
  blocking collectives  385 us (44%)
  local copies, waits for them, and re-layouts  350 us (40%)
  other arithmetic  52.8 us (6%)
  loops' own time  33 us (4%)
  matrix products  25.5 us (3%)
  starting transfers between devices  12.6 us (1%)
    psum x1, blocking collectives, per_device(): lax.psum((weight_acc, bias_acc), ('face', 'tile', 'dp'))  385 us
    reshape x27, local copies, waits for them, and re-layouts, step(): patch_grad[:, start:start + channels]  126 us
    reshape x3, local copies, waits for them, and re-layouts, unfold(): return jnp.concatenate(parts, -1).reshape(-1, 9 * channels)  37.1 us
    another operation x1, loops' own time, per_device(): lax.fori_loop(0, wet_total, step, initial)  33 us
    while x30, local copies, waits for them, and re-layouts  28.6 us
    unnamed x73, local copies, waits for them, and re-layouts  27.8 us
    another operation x3, other arithmetic  21.4 us
  transfers between devices with their start and end apart: 8, of which 0 were waited for; matrix products, arithmetic and copies ran while one was open for 4% of the time, Pallas kernels for 0%

commit v1 on v0

v1 whole, which is shorter than its diff:
```python
import functools
import math

import jax
import jax.numpy as jnp
import ml_dtypes
import numpy as np
from jax import lax
from jax.experimental import pallas as pl
from jax.experimental.pallas import tpu as pltpu
from jax.sharding import PartitionSpec as P

MESH = pl.DeviceIdType.MESH
BF = jnp.bfloat16
F32 = jnp.float32
T = 90
C = 32
SL = 6
G = 96
R = SL * G
W = T * C
WP = 3072
NB = 12
LAST = W - 11 * 256
VMEM_LIMIT = 62 * 2**20


def spread_matrix():
    m = np.zeros((256, WP), np.float32)
    for j in range(T):
        m[j, j * C : (j + 1) * C] = 1
        m[128 + j, j * C : (j + 1) * C] = 1
    return m.astype(ml_dtypes.bfloat16)


def flip_lanes_matrix():
    m = np.zeros((256, 128), np.float32)
    for q in range(4):
        for k in range(C):
            m[C * (5 - q) + k, C * q + k] = 1
    return m.astype(ml_dtypes.bfloat16)


def flip_rows_matrix():
    m = np.zeros((G, G), np.float32)
    for i in range(T):
        m[i, T - 1 - i] = 1
    return m.astype(ml_dtypes.bfloat16)


def dot(a, b):
    return jnp.dot(a, b, preferred_element_type=F32)


def dot_t(a, b):
    return lax.dot_general(a, b, (((1,), (1,)), ((), ())), preferred_element_type=F32)


def split_hi_lo(v):
    hi = v.astype(BF)
    lo = (v - hi.astype(F32)).astype(BF)
    return hi, lo


def edge_kernel(
    xr0, xr1, xc0, xc1, gr0, gr1, gc0, gc1, wa, spread, r0_out, r1_out, c0_out, c1_out
):
    def rows_of(ref, row):
        parts = [ref[0, s, row : row + 1, :].astype(F32) for s in range(SL)]
        v = jnp.concatenate(parts + [jnp.zeros((2, W), F32)], 0)
        return jnp.concatenate([v, jnp.zeros((8, WP - W), F32)], 1)

    area = jnp.concatenate(
        [wa[s, 0:1, :] for s in range(SL)]
        + [jnp.zeros((2, T), F32)]
        + [wa[s, T - 1 : T, :] for s in range(SL)]
        + [jnp.zeros((2, T), F32)],
        0,
    )
    area = jnp.concatenate([area, jnp.zeros((16, 128 - T), F32)], 1)
    hi, lo = split_hi_lo(area)
    wide = dot(jnp.concatenate([hi, lo], 1), spread[...])
    for row, x_ref, g_ref, e, out in (
        (0, xr0, gr0, wide[0:8], r0_out),
        (T - 1 - 80, xr1, gr1, wide[8:16], r1_out),
    ):
        xv = jnp.where(e > 0, rows_of(x_ref, row), 0.0)
        gv = jnp.where(e > 0, e * rows_of(g_ref, row), 0.0)
        out[...] = jnp.concatenate([xv, gv], 0).astype(BF)
    pad = jnp.zeros((G - T, 128), BF)
    for lane, col, x_ref, g_ref, out in ((0, 0, xc0, gc0, c0_out), (C, T - 1, xc1, gc1, c1_out)):
        for s in range(SL):
            e = jnp.broadcast_to(wa[s, :, col : col + 1], (T, C))
            xv = jnp.where(e > 0, x_ref[0, s, :, lane : lane + C].astype(F32), 0.0)
            gv = jnp.where(e > 0, e * g_ref[0, s, :, lane : lane + C].astype(F32), 0.0)
            v = jnp.concatenate([xv, gv, jnp.zeros((T, 64), F32)], 1).astype(BF)
            out[s * G : (s + 1) * G] = jnp.concatenate([v, pad], 0)


def edges(x, g, wa, spread):
    row_lo = pl.BlockSpec((1, SL, 16, W), lambda i: (0, 0, 0, 0))
    row_hi = pl.BlockSpec((1, SL, 16, W), lambda i: (0, 0, 5, 0))
    col_lo = pl.BlockSpec((1, SL, T, 128), lambda i: (0, 0, 0, 0))
    col_hi = pl.BlockSpec((1, SL, T, 128), lambda i: (0, 0, 0, 22))

    def whole(shape):
        return pl.BlockSpec(shape, lambda i: (0,) * len(shape))

    return pl.pallas_call(
        edge_kernel,
        grid=(1,),
        in_specs=[row_lo, row_hi, col_lo, col_hi] * 2
        + [whole((SL, T, T)), whole((256, WP))],
        out_specs=[whole((16, WP))] * 2 + [whole((R, 128))] * 2,
        out_shape=[jax.ShapeDtypeStruct((16, WP), BF)] * 2
        + [jax.ShapeDtypeStruct((R, 128), BF)] * 2,
        compiler_params=pltpu.CompilerParams(vmem_limit_bytes=40 * 2**20),
    )(x, x, x, x, g, g, g, g, wa, spread)


def main_kernel(
    nb,
    rev,
    x_hbm,
    g_hbm,
    wa,
    spread,
    flip_l,
    flip_r,
    weight,
    bias,
    ra,
    rb,
    ca,
    cb,
    y_hbm,
    gi_hbm,
    part_out,
    xs,
    gs,
    x3,
    s3,
    xp,
    qx,
    qs,
    wet,
    cols,
    in_sem,
    out_sem,
):
    yo, go = xs, gs
    copies = []
    for s in range(SL):
        copies.append(pltpu.make_async_copy(x_hbm.at[0, s], xs.at[s], in_sem.at[0, s]))
        copies.append(pltpu.make_async_copy(g_hbm.at[0, s], gs.at[s], in_sem.at[1, s]))
    for copy in copies:
        copy.start()

    w = weight[...].astype(F32)

    def tap(a, c):
        start = (3 * a + c) * C
        return w[start : start + C]

    def band(a, cells_in, shift, mirror=False):
        rows_iota = lax.broadcasted_iota(jnp.int32, (256, cells_in * C), 0) // C
        lanes_iota = lax.broadcasted_iota(jnp.int32, (256, cells_in * C), 1) // C - shift
        which = rows_iota - lanes_iota + 1
        if mirror:
            which = 2 - which
        out = jnp.zeros((256, cells_in * C), F32)
        for c in range(3):
            wide = jnp.concatenate([tap(a, c)] * 4, 1)
            wide = jnp.concatenate([wide] * (cells_in // 4), 1)
            out = jnp.where(which == c, jnp.concatenate([wide] * 8, 0), out)
        return out.astype(BF)

    bands = [band(a, 8, 0) for a in range(3)]
    z32 = jnp.zeros((C, C), F32)
    z64 = jnp.zeros((C, 192), F32)
    wq_rows = []
    for slot in (0, None, 1, 2):
        if slot is None:
            continue
        wq_rows.append(jnp.concatenate([tap(slot, 0), z32, z64], 1))
        wq_rows.append(jnp.concatenate([z64, z32, tap(slot, 2)], 1))
    wq = jnp.concatenate(wq_rows + [jnp.zeros((64, 256), F32)], 0).astype(BF)
    gl = jnp.concatenate(
        [v for a in range(3) for v in (tap(2 - a, 2), z32)] + [z32, z32], 1
    )
    gr = jnp.concatenate(
        [v for a in range(3) for v in (z32, tap(2 - a, 0))] + [z32, z32], 1
    )
    wqb = jnp.concatenate([gl, jnp.zeros((192, 256), F32), gr], 0).astype(BF)

    zr = jnp.concatenate([ra[...], rb[...]], 0)
    zpad = jnp.concatenate([jnp.zeros((32, 128), BF), zr], 1)
    stacked = jnp.concatenate(
        [zpad[:, 128 * (22 - n) : 128 * (24 - n)] for n in range(23)], 0
    )
    turned = dot(stacked, flip_l[...]).astype(BF)
    flipped = jnp.concatenate(
        [turned[32 * n : 32 * n + 32] for n in range(23)] + [jnp.zeros((32, 128), BF)], 1
    )
    lane_i = lax.broadcasted_iota(jnp.int32, (128, 64), 1)
    row_i = lax.broadcasted_iota(jnp.int32, (128, 64), 0)
    sel = jnp.zeros((128, 64), F32)
    for s in range(SL):
        for side, halo_row in ((0, (16 * (s - 1) + 15) % 96), (1, 16 * s + 10)):
            n, r = nb[s, side], rev[s, side]
            src = 16 * side + 32 * r + lax.rem(jnp.maximum(n, 0), SL)
            src = jnp.where(n >= 0, src, -100)
            sel = jnp.where((row_i == halo_row) & (lane_i == src), 1.0, sel)
            rim_row = 96 + 16 * side + 8 * r + s
            sel = jnp.where((row_i == rim_row) & (lane_i == src + 8), 1.0, sel)
    routed = dot(sel.astype(BF), jnp.concatenate([zr, flipped], 0))
    hx = routed[0:96]
    hs = routed[96:128].astype(BF)
    hs = jnp.concatenate(
        [jnp.zeros((32, 128), BF), hs, jnp.zeros((32, 128), BF)], 1
    )
    rim = []
    for side, a in ((0, 2), (1, 0)):
        total = None
        for r in range(2):
            rows = hs[16 * side + 8 * r : 16 * side + 8 * r + 8].astype(F32)
            lhs = jnp.concatenate(
                [rows[:, 256 * m : 256 * m + 512] for m in range(NB)], 0
            ).astype(BF)
            part = dot_t(lhs, band(a, 16, 4, mirror=(r == 1)))
            total = part if total is None else total + part
        rim.append(total.astype(BF).astype(F32))

    for side, ref in ((0, ca), (1, cb)):
        flat = jnp.concatenate([ref[s * G : (s + 1) * G] for s in range(SL)], 1)
        back = dot(flip_r[...], flat)
        for s in range(SL):
            cols[side, 0, s] = ref[s * G : (s + 1) * G].astype(F32)
            cols[side, 1, s] = back[:, 128 * s : 128 * s + 128]
    ecol, xleft, xright = [], [], []
    for s in range(SL):
        got = []
        pieces = []
        for side in range(2):
            n, r = nb[s, 2 + side], rev[s, 2 + side]
            v = cols[side, r, lax.rem(jnp.maximum(n, 0), SL)]
            v = jnp.where(n >= 0, v, 0.0)
            got.append(v)
            pieces.append(jnp.where(r == 0, v, 0.0)[:, C : 2 * C])
            pieces.append(jnp.where(r == 1, v, 0.0)[:, C : 2 * C])
        ecol.append(jnp.concatenate(pieces, 1))
        xright.append(got[0])
        xleft.append(got[1])
    ecol = jnp.concatenate(ecol, 0)
    xright = jnp.concatenate(xright, 0)
    xleft = jnp.concatenate(xleft, 0)
    e3 = jnp.concatenate(
        [pltpu.roll(ecol, 1, 0), ecol, pltpu.roll(ecol, R - 1, 0)], 1
    ).astype(BF)
    v2 = jnp.concatenate(
        [v for a in range(3) for v in (tap(2 - a, 0), tap(a, 0), z32, z32)], 1
    )
    v3 = jnp.concatenate(
        [v for a in range(3) for v in (z32, z32, tap(2 - a, 2), tap(a, 2))], 1
    )
    rim_col = dot_t(e3, jnp.concatenate([v2, v3], 0).astype(BF)).astype(BF).astype(F32)
    zc = jnp.zeros((R, C), F32)
    z6 = jnp.zeros((R, 192), F32)
    rim_first = jnp.concatenate([rim_col[:, C : 2 * C], zc, z6], 1)
    rim_last = jnp.concatenate([zc, rim_col[:, 0:C], z6], 1)
    halo_right = jnp.concatenate([zc, zc, xright[:, 0:C], jnp.zeros((R, 160), F32)], 1)
    xleft = xleft[:, 0:C].astype(BF)

    area = []
    for s in range(SL):
        v = jnp.concatenate([wa[s], jnp.zeros((G - T, T), F32)], 0)
        area.append(jnp.concatenate([v, jnp.zeros((G, 128 - T), F32)], 1))
    hi, lo = split_hi_lo(jnp.concatenate(area, 0))
    area = jnp.concatenate([hi, lo], 1)

    for copy in copies:
        copy.wait()

    def fetch(ref, m):
        parts = []
        for s in range(SL):
            lanes = LAST if m == NB - 1 else 256
            v = ref[s, :, 256 * m : 256 * m + lanes].astype(F32)
            if lanes < 256:
                v = jnp.concatenate([v, jnp.zeros((T, 256 - lanes), F32)], 1)
            parts.append(v)
            parts.append(jnp.zeros((G - T, 256), F32))
        return jnp.concatenate(parts, 0)

    def down(v):
        return jnp.concatenate([v[R - 1 :], v[: R - 1]], 0)

    def up(v):
        return jnp.concatenate([v[1:], v[:1]], 0)

    bias_acc = jnp.zeros((8, 256), F32)
    for m in range(NB):
        blk = slice(256 * m, 256 * m + 256)
        e = dot(area, spread[:, blk])
        wet[:, blk] = (e > 0).astype(F32).astype(BF)
        xv = jnp.where(e > 0, fetch(xs, m), 0.0)
        parts = []
        for s in range(SL):
            parts.append(xv[G * s : G * s + 80])
            parts.append(xv[G * s + 80 : G * s + 96] + hx[16 * s : 16 * s + 16, blk])
        xv = jnp.concatenate(parts, 0)
        if m == NB - 1:
            xv = xv + halo_right
        xv = xv.astype(BF)
        x3[0, :, blk] = down(xv)
        x3[1, :, blk] = xv
        x3[2, :, blk] = up(xv)
        sv = jnp.where(e > 0, e * fetch(gs, m), 0.0).astype(BF)
        s3[0, :, blk] = down(sv)
        s3[1, :, blk] = sv
        s3[2, :, blk] = up(sv)
        bias_acc = bias_acc + jnp.sum(sv.astype(F32).reshape(R // 8, 8, 256), 0)

    zb = jnp.zeros((R, C), BF)
    lane128 = lax.broadcasted_iota(jnp.int32, (R, 128), 1)
    for m in range(NB):
        for ref, out, first in ((x3, qx, xleft), (s3, qs, zb)):
            left = first if m == 0 else ref[1, :, 256 * m - 128 : 256 * m][:, 96:128]
            right = zb if m == NB - 1 else ref[1, :, 256 * m + 256 : 256 * m + 384][:, 0:C]
            q = jnp.concatenate([left, right, left, right], 1)
            out[:, 256 * m : 256 * m + 128] = jnp.where(lane128 < 64, down(q), q)
            out[:, 256 * m + 128 : 256 * m + 256] = up(q)
    for n in range(24):
        left = xleft if n == 0 else x3[1, :, 128 * (n - 1) : 128 * n][:, 96:128]
        xp[:, 128 * n : 128 * n + 128] = jnp.concatenate(
            [left, x3[1, :, 128 * n : 128 * n + 128][:, 0:96]], 1
        )

    bias_row = jnp.concatenate([bias[...]] * 8, 1)
    out_copies = []
    for m in range(NB):
        blk = slice(256 * m, 256 * m + 256)
        y = dot(x3[0, :, blk], bands[0]) + dot(x3[1, :, blk], bands[1])
        y = y + dot(x3[2, :, blk], bands[2]) + dot(qx[:, blk], wq) + bias_row
        y = (y * wet[:, blk].astype(F32)).astype(BF)
        lanes = LAST if m == NB - 1 else 256
        for s in range(SL):
            yo[s, :, 256 * m : 256 * m + lanes] = y[G * s : G * s + T, :lanes]
    for s in range(SL):
        out_copies.append(pltpu.make_async_copy(yo.at[s], y_hbm.at[0, s], out_sem.at[0, s]))
        out_copies[-1].start()

    row8 = lax.broadcasted_iota(jnp.int32, (8, 256), 0)
    for m in range(NB):
        blk = slice(256 * m, 256 * m + 256)
        y = dot_t(s3[0, :, blk], bands[2]) + dot_t(s3[1, :, blk], bands[1])
        y = y + dot_t(s3[2, :, blk], bands[0]) + dot_t(qs[:, blk], wqb)
        if m == 0:
            y = y + rim_first
        if m == NB - 1:
            y = y + rim_last
        parts = []
        for s in range(SL):
            top = jnp.where(row8 == 0, rim[0][8 * m + s : 8 * m + s + 1], 0.0)
            low = jnp.where(row8 == 1, rim[1][8 * m + s : 8 * m + s + 1], 0.0)
            parts.append(y[G * s : G * s + 8] + top)
            parts.append(y[G * s + 8 : G * s + 88])
            parts.append(y[G * s + 88 : G * s + 96] + low)
        y = jnp.concatenate(parts, 0)
        y = (y * wet[:, blk].astype(F32)).astype(BF)
        lanes = LAST if m == NB - 1 else 256
        for s in range(SL):
            go[s, :, 256 * m : 256 * m + lanes] = y[G * s : G * s + T, :lanes]
    for s in range(SL):
        out_copies.append(pltpu.make_async_copy(go.at[s], gi_hbm.at[0, s], out_sem.at[1, s]))
        out_copies[-1].start()

    grad = jnp.zeros((384, 256), F32)
    for m in range(23):
        sv = jnp.concatenate(
            [s3[2 - a, :, 128 * m : 128 * m + 128] for a in range(3)], 1
        )
        xv = xp[:, 128 * m : 128 * m + 256]
        grad = grad + lax.dot_general(
            sv, xv, (((0,), (0,)), ((), ())), preferred_element_type=F32
        )
    for a in range(3):
        total = None
        for j in range(4):
            piece = grad[128 * a + C * j : 128 * a + C * j + C, C * j : C * j + 96]
            total = piece if total is None else total + piece
        part_out[C * a : C * a + C] = jnp.concatenate([total, jnp.zeros((C, C), F32)], 1)
    row = jnp.sum(bias_acc, 0, keepdims=True)
    row = row[:, 0:128] + row[:, 128:256]
    row = row[:, 0:64] + row[:, 64:128]
    row = row[:, 0:C] + row[:, C : 2 * C]
    low = jnp.concatenate([row, jnp.zeros((1, 96), F32)], 1)
    part_out[96:128] = jnp.concatenate([low, jnp.zeros((31, 128), F32)], 0)
    for copy in out_copies:
        copy.wait()


def local_part(x, g, wa, consts, weight, bias, got, neighbours, reversal):
    any_ = pl.BlockSpec(memory_space=pl.ANY)
    vm = pl.BlockSpec(memory_space=pltpu.VMEM)
    sm = pl.BlockSpec(memory_space=pltpu.SMEM)
    tiles = jax.ShapeDtypeStruct((1, SL, T, W), BF)
    return pl.pallas_call(
        main_kernel,
        in_specs=[sm, sm, any_, any_] + [vm] * 10,
        out_specs=[any_, any_, vm],
        out_shape=[tiles, tiles, jax.ShapeDtypeStruct((128, 128), F32)],
        scratch_shapes=[
            pltpu.VMEM((SL, T, W), BF),
            pltpu.VMEM((SL, T, W), BF),
            pltpu.VMEM((3, R, WP), BF),
            pltpu.VMEM((3, R, WP), BF),
            pltpu.VMEM((R, WP), BF),
            pltpu.VMEM((R, WP), BF),
            pltpu.VMEM((R, WP), BF),
            pltpu.VMEM((R, WP), BF),
            pltpu.VMEM((2, 2, SL, G, 128), F32),
            pltpu.SemaphoreType.DMA((2, SL)),
            pltpu.SemaphoreType.DMA((2, SL)),
        ],
        compiler_params=pltpu.CompilerParams(vmem_limit_bytes=VMEM_LIMIT),
    )(neighbours, reversal, x, g, wa, *consts, weight, bias, *got)


def sum_kernel(n_face, n_tile, n_dp, scale, p_ref, w_out, b_out, got1, mine, got2, full, s1, r1, s2, r2, s3, r3):
    f, t, d = lax.axis_index("face"), lax.axis_index("tile"), lax.axis_index("dp")
    n_plane = n_face * n_dp
    me = f * n_dp + d

    def tile_peer(k):
        return (f, lax.rem(t + k, n_tile), d)

    def plane_peer(k):
        q = lax.rem(me + k, n_plane)
        return (q // n_dp, t, lax.rem(q, n_dp))

    barrier = pltpu.get_barrier_semaphore()
    for k in range(1, n_tile):
        pl.semaphore_signal(barrier, inc=1, device_id=tile_peer(k), device_id_type=MESH)
    for k in range(1, n_plane):
        pl.semaphore_signal(barrier, inc=1, device_id=plane_peer(k), device_id_type=MESH)
    pl.semaphore_wait(barrier, n_tile + n_plane - 2)

    def rows8(i):
        return pl.ds(pl.multiple_of(i * 8, 8), 8)

    sends = []
    for k in range(1, n_tile):
        u = lax.rem(t + k, n_tile)
        copy = pltpu.make_async_remote_copy(
            src_ref=p_ref.at[rows8(u)],
            dst_ref=got1.at[k],
            send_sem=s1.at[k],
            recv_sem=r1.at[k],
            device_id=tile_peer(k),
            device_id_type=MESH,
        )
        copy.start()
        sends.append(copy)
    got1[0] = p_ref[rows8(t)]
    for copy in sends:
        copy.wait()
    total = got1[0]
    for k in range(1, n_tile):
        total = total + got1[k]
    mine[...] = total

    sends = []
    for k in range(1, n_plane):
        copy = pltpu.make_async_remote_copy(
            src_ref=mine,
            dst_ref=got2.at[me],
            send_sem=s2.at[k],
            recv_sem=r2.at[k],
            device_id=plane_peer(k),
            device_id_type=MESH,
        )
        copy.start()
        sends.append(copy)
    got2[me] = mine[...]
    for copy in sends:
        copy.wait()
    total = got2[0]
    for k in range(1, n_plane):
        total = total + got2[k]
    full[rows8(t)] = total * scale

    sends = []
    for k in range(1, n_tile):
        copy = pltpu.make_async_remote_copy(
            src_ref=full.at[rows8(t)],
            dst_ref=full.at[rows8(t)],
            send_sem=s3.at[k],
            recv_sem=r3.at[k],
            device_id=tile_peer(k),
            device_id_type=MESH,
        )
        copy.start()
        sends.append(copy)
    for copy in sends:
        copy.wait()
    for a in range(3):
        w_out[96 * a : 96 * a + 96] = full[C * a : C * a + C].T[0:96]
    b_out[...] = full[96:97, 0:C]


def device_sum(part, n_face, n_tile, n_dp, scale):
    vm = pl.BlockSpec(memory_space=pltpu.VMEM)
    n_plane = n_face * n_dp
    dma = pltpu.SemaphoreType.DMA
    return pl.pallas_call(
        functools.partial(sum_kernel, n_face, n_tile, n_dp, scale),
        in_specs=[vm],
        out_specs=[vm, vm],
        out_shape=[
            jax.ShapeDtypeStruct((9 * C, C), F32),
            jax.ShapeDtypeStruct((1, C), F32),
        ],
        scratch_shapes=[
            pltpu.VMEM((n_tile, 8, 128), F32),
            pltpu.VMEM((8, 128), F32),
            pltpu.VMEM((n_plane, 8, 128), F32),
            pltpu.VMEM((128, 128), F32),
            dma((n_tile,)),
            dma((n_tile,)),
            dma((n_plane,)),
            dma((n_plane,)),
            dma((n_tile,)),
            dma((n_tile,)),
        ],
        compiler_params=pltpu.CompilerParams(collective_id=0, has_side_effects=True),
    )(part)


def passed_along(block, axis, distance):
    n = lax.axis_size(axis)
    return lax.ppermute(block, axis, [((i - distance) % n, i) for i in range(n)])


def per_device(
    inputs, cotangent, conv_weight, out_bias, cell_area, land_mask, neighbours, reversal, wet_count
):
    occupied = jnp.arange(SL, dtype=jnp.int32) < wet_count[0]
    wa = jnp.where((land_mask != 0) & occupied[:, None], cell_area, 0.0).reshape(SL, T, T)
    spread = jnp.asarray(spread_matrix())
    flip_l = jnp.asarray(flip_lanes_matrix())
    flip_r = jnp.asarray(flip_rows_matrix())
    r0, r1, c0, c1 = edges(inputs, cotangent, wa, spread)
    got = (
        passed_along(r1, "tile", -1),
        passed_along(r0, "tile", 1),
        passed_along(c0, "face", -1),
        passed_along(c1, "face", 1),
    )
    outputs, input_grad, part = local_part(
        inputs,
        cotangent,
        wa,
        (spread, flip_l, flip_r),
        conv_weight,
        out_bias[None],
        got,
        neighbours,
        reversal,
    )
    n_face, n_tile, n_dp = (lax.axis_size(a) for a in ("face", "tile", "dp"))
    scale = 1.0 / math.sqrt(n_dp * n_face * n_tile * SL * T * T)
    weight_grad, bias_grad = device_sum(part, n_face, n_tile, n_dp, scale)
    return outputs, input_grad, weight_grad, bias_grad[0]


def solution(mesh):
    return jax.shard_map(
        per_device,
        mesh=mesh,
        in_specs=(
            P("dp", ("face", "tile"), None, None),
            P("dp", ("face", "tile"), None, None),
            P(),
            P(),
            P(("face", "tile"), None),
            P(("face", "tile"), None),
            P(("face", "tile"), None),
            P(("face", "tile"), None),
            P(("face", "tile")),
        ),
        out_specs=(
            P("dp", ("face", "tile"), None, None),
            P("dp", ("face", "tile"), None, None),
            P(),
            P(),
        ),
        check_vma=False,
    )
```

time: 870 us -> 77.7 us (0.09)
  blocking collectives: 385 us -> 0 us
  local copies, waits for them, and re-layouts: 350 us -> 11.3 us
  Pallas kernels: 0 us -> 55.5 us
  other arithmetic: 52.8 us -> 1.14 us
  loops' own time: 33 us -> 0 us
  matrix products: 25.5 us -> 0 us
    psum x1 -> x0, blocking collectives: 385 us -> none  [per_device(): lax.psum((weight_acc, bias_acc), ('face', 'tile', 'dp'))]
    reshape x52 -> x1, local copies, waits for them, and re-layouts: 176 us -> 0.39 us  [per_device(): jnp.where((land_mask != 0) & occupied[:, None], cell_area, 0.0)]
    pallas_call x0 -> x3, Pallas kernels: none -> 55.5 us  [the longest x1 28.4 us: local_part(): pl.pallas_call(main_kernel, in_specs=[sm, sm, any_, any_] + [vm] * 10, ou...]
    broadcast_in_dim x13 -> x0, local copies, waits for them, and re-layouts: 41 us -> none  [the longest x1 8.1 us: per_device(): returned[0].astype(jnp.float32)[:, :, None]]
    another operation x1 -> x0, loops' own time: 33 us -> none  [per_device(): lax.fori_loop(0, wet_total, step, initial)]
    while x30 -> x0, local copies, waits for them, and re-layouts: 28.6 us -> none
    dot_general x9 -> x0, matrix products: 25.5 us -> none  [the longest x3 11.4 us: step(): lax.dot_general(patches, flat_grad, (((0,), (0,)), ((), ())), preferred_e...]
    slice x18 -> x0, local copies, waits for them, and re-layouts: 24.2 us -> none  [the longest x3 10.1 us: step(): patch_grad[:, start:start + channels]]
  transfers between devices with their start and end apart: 8 -> 4, of which waited for: 0 -> 2; matrix products, arithmetic and copies ran while one was open for 4% -> 3% of each run, Pallas kernels for 0% -> 0%
where the time goes in v1:
time: 77.7 us; the launch traced here: 77.3 us
  Pallas kernels  55.5 us (71%)
  local copies, waits for them, and re-layouts  11.3 us (15%)
  starting transfers between devices  5.87 us (8%)
  waiting for transfers between devices  2.19 us (3%)
  between operations  1.37 us (2%)
  other arithmetic  1.14 us (1%)
    pallas_call x1, Pallas kernels, local_part(): pl.pallas_call(main_kernel, in_specs=[sm, sm, any_, any_] + [vm] * 10, ou...  28.4 us
    pallas_call x1, Pallas kernels, device_sum(): pl.pallas_call(functools.partial(sum_kernel, n_face, n_tile, n_dp, scale)...  26.2 us
    unnamed x27, local copies, waits for them, and re-layouts  10.9 us
    ppermute x4, starting transfers between devices, passed_along(): lax.ppermute(block, axis, [((i - distance) % n, i) for i in range(n)])  5.87 us
    ppermute x4, waiting for transfers between devices, passed_along(): lax.ppermute(block, axis, [((i - distance) % n, i) for i in range(n)])  2.19 us
  transfers between devices with their start and end apart: 4, of which 2 were waited for; matrix products, arithmetic and copies ran while one was open for 3% of the time, Pallas kernels for 0%

profile of v1, /device:TPU:1, one launch (start us, length us, event | category | flops | bytes accessed | tf_op | source)
XLA Modules:
  0.0 77.3 jit_solution(7590237768820334478)
XLA Ops:
  1.3 1.1 %and_select_fusion = f32[6,8100]{1,0:T(8,128)S(1)} fusion(f32[6,8100]{1,0:T(8,128)} %param.16, s32[6,8100]{1,0:T(8,128)} %param.17, pred[6]{0:T(512)(128)(4,1)S(1)} %iota_compare_fusion), kind=kLoop, calls=%fused_computation | loop fusion | flops 145800 | bytes 583206 | tf_op jit(solution)/shard_map/jit(_where)/select_n | solution.py:549
  2.4 0.4 reshape.15.wa
  2.8 0.0 copy-start
  2.8 2.0 %copy-done = bf16[1,6,90,2880]{3,2,1,0:T(8,128)(2,1)S(1)} copy-done((bf16[1,6,90,2880]{3,2,1,0:T(8,128)(2,1)S(1)}, bf16[1,6,90,2880]{3,2,1,0:T(8,128)(2,1)}, u32[]{:S(2)}) %copy-start) | copy-done | bytes 3110424
  4.8 0.0 copy-start.1
  4.8 2.0 %copy-done.1 = bf16[1,6,90,2880]{3,2,1,0:T(8,128)(2,1)S(1)} copy-done((bf16[1,6,90,2880]{3,2,1,0:T(8,128)(2,1)S(1)}, bf16[1,6,90,2880]{3,2,1,0:T(8,128)(2,1)}, u32[]{:S(2)}) %copy-start.1) | copy-done | bytes 3110424
  6.7 1.4 %copy-done.2 = bf16[256,3072]{1,0:T(8,128)(2,1)S(1)} copy-done((bf16[256,3072]{1,0:T(8,128)(2,1)S(1)}, bf16[256,3072]{1,0:T(8,128)(2,1)}, u32[]{:S(2)}) %copy-start.2) | copy-done | bytes 1572888
  8.2 0.9 %shard_map.147 = (bf16[16,3072]{1,0:T(8,128)(2,1)S(1)}, bf16[16,3072]{1,0:T(8,128)(2,1)S(1)}, bf16[576,128]{1,0:T(8,128)(2,1)S(1)}, bf16[576,128]{1,0:T(8,128)(2,1)S(1)}) custom-call(bf16[1,6,90,2880]{3,2,1,0:T(8,128)(2,1)S(1)} %copy-done, bf16[1,6,90,2880]{3,2,1,0:T(8,128)(2,1)S(1)} %copy-done, bf16[1,6,90,2880]{3,2,1,0:T(8,128)(2,1)S(1)} %copy-done, ...), custom_call_target="tpu_custom_call" | custom-call | tf_op jit(solution)/shard_map/pallas_call | solution.py:109
  9.1 0.0 copy-done.3
  9.1 3.4 %collective-permute-start.2 = (bf16[576,128]{1,0:T(8,128)(2,1)S(1)}, bf16[576,128]{1,0:T(8,128)(2,1)S(1)}, u32[]{:S(2)}, u32[]{:S(2)}) collective-permute-start(bf16[576,128]{1,0:T(8,128)(2,1)S(1)} %get-tuple-element.15), channel_id=1, source_target_pairs={{64,0},{128,64},{192,128},{0,192},{65,1},{129,65},{193,129},{1,193... | collective-permute-start | bytes 442376 | tf_op jit(solution)/shard_map/ppermute | solution.py:542
  12.5 0.0 collective-permute-start.3
  12.5 2.0 %collective-permute-start = (bf16[16,3072]{1,0:T(8,128)(2,1)S(1)}, bf16[16,3072]{1,0:T(8,128)(2,1)S(1)}, u32[]{:S(2)}, u32[]{:S(2)}) collective-permute-start(bf16[16,3072]{1,0:T(8,128)(2,1)S(1)} %get-tuple-element.13), channel_id=1, source_target_pairs={{4,0},{8,4},{12,8},{16,12},{20,16},{24,20},{28,24},{32,28},{36,32}... | collective-permute-start | bytes 294920 | tf_op jit(solution)/shard_map/ppermute | solution.py:542
  14.4 0.5 collective-permute-start.1
  15.0 0.0 copy-done.9
  15.0 0.7 copy.16.nb
  15.6 0.0 copy-done.10
  15.7 0.7 copy.17.rev
  16.3 0.0 copy-done.8
  16.3 0.7 copy.18.weight
  17.1 0.2 collective-permute-done.ra
  17.3 2.0 %collective-permute-done.1.rb = bf16[16,3072]{1,0:T(8,128)(2,1)S(1)} collective-permute-done((bf16[16,3072]{1,0:T(8,128)(2,1)S(1)}, bf16[16,3072]{1,0:T(8,128)(2,1)S(1)}, u32[]{:S(2)}, u32[]{:S(2)}) %collective-permute-start.1) | collective-permute-done | bytes 98336 | tf_op jit(solution)/shard_map/ppermute | solution.py:542
  19.3 0.0 collective-permute-done.2.ca
  19.3 0.0 collective-permute-done.3.cb
  19.3 0.0 copy-start.5
  19.3 0.0 copy-done.6
  19.3 0.6 copy-done.7
  19.9 0.1 copy-done.4
  19.9 0.1 copy-done.5
  20.0 28.4 %shard_map.148 = (bf16[1,6,90,2880]{3,2,1,0:T(8,128)(2,1)}, bf16[1,6,90,2880]{3,2,1,0:T(8,128)(2,1)}, f32[128,128]{1,0:T(8,128)}) custom-call(s32[6,4]{1,0:T(8,128)} %copy.16.nb, s32[6,4]{1,0:T(8,128)} %copy.17.rev, bf16[1,6,90,2880]{3,2,1,0:T(8,128)(2,1)} %x_hbm.1, bf16[1,6,90,2880]{3,2,1,0:T(8,128)(2,1)} %g_hbm.1, f32[6,90,90]{2,1,0:T(8,128)} %copy-done.3, ...), custom_call_target="tpu_custom_call" | custom-call | tf_op jit(solution)/shard_map/pallas_call | solution.py:408
  48.4 26.2 %shard_map.149 = (f32[288,32]{1,0:T(8,128)}, f32[1,32]{1,0:T(1,128)}) custom-call(f32[128,128]{1,0:T(8,128)} %get-tuple-element.19.p_ref), custom_call_target="tpu_custom_call" | custom-call | tf_op jit(solution)/shard_map/pallas_call | solution.py:516
  74.6 1.6 %copy.19 = f32[288,32]{0,1:T(8,128)} copy(f32[288,32]{1,0:T(8,128)} %get-tuple-element.24) | data formatting | bytes 73728
  76.2 1.1 %copy.22 = f32[32]{0:T(128)} copy(f32[32]{0:T(128)} %bitcast.5) | data formatting | bytes 256
  (9 shorter events, 0.0 us)
Async XLA Ops:
  2.8 2.0 %copy-start = (bf16[1,6,90,2880]{3,2,1,0:T(8,128)(2,1)S(1)}, bf16[1,6,90,2880]{3,2,1,0:T(8,128)(2,1)}, u32[]{:S(2)}) copy-start(bf16[1,6,90,2880]{3,2,1,0:T(8,128)(2,1)} %x_hbm.1) | copy-start | bytes 9331204
  4.8 2.0 %copy-start.1 = (bf16[1,6,90,2880]{3,2,1,0:T(8,128)(2,1)S(1)}, bf16[1,6,90,2880]{3,2,1,0:T(8,128)(2,1)}, u32[]{:S(2)}) copy-start(bf16[1,6,90,2880]{3,2,1,0:T(8,128)(2,1)} %g_hbm.1) | copy-start | bytes 9331204
  6.7 1.4 %copy-start.2 = (bf16[256,3072]{1,0:T(8,128)(2,1)S(1)}, bf16[256,3072]{1,0:T(8,128)(2,1)}, u32[]{:S(2)}) copy-start(bf16[256,3072]{1,0:T(8,128)(2,1)} %constant.10.clone.spread) | copy-start | bytes 4718596
  8.2 0.9 %copy-start.3 = (f32[6,90,90]{2,1,0:T(8,128)}, f32[6,90,90]{2,1,0:T(8,128)S(1)}, u32[]{:S(2)}) copy-start(f32[6,90,90]{2,1,0:T(8,128)S(1)} %reshape.15.wa) | copy-start | bytes 583204
  8.2 6.8 %copy-start.9 = (s32[6,4]{0,1:T(4,128)S(1)}, s32[6,4]{0,1:T(4,128)}, u32[]{:S(2)}) copy-start(s32[6,4]{0,1:T(4,128)} %param.18) | copy-start | bytes 292
  8.2 7.5 %copy-start.10 = (s32[6,4]{0,1:T(4,128)S(1)}, s32[6,4]{0,1:T(4,128)}, u32[]{:S(2)}) copy-start(s32[6,4]{0,1:T(4,128)} %param.19) | copy-start | bytes 292
  8.2 8.2 %copy-start.8 = (bf16[288,32]{0,1:T(8,128)(2,1)S(1)}, bf16[288,32]{0,1:T(8,128)(2,1)}, u32[]{:S(2)}) copy-start(bf16[288,32]{0,1:T(8,128)(2,1)} %param.14) | copy-start | bytes 55300
  9.1 10.2 %collective-permute-start.2 = (bf16[576,128]{1,0:T(8,128)(2,1)S(1)}, bf16[576,128]{1,0:T(8,128)(2,1)S(1)}, u32[]{:S(2)}, u32[]{:S(2)}) collective-permute-start(bf16[576,128]{1,0:T(8,128)(2,1)S(1)} %get-tuple-element.15), channel_id=1, source_target_pairs={{64,0},{128,64},{192,128},{0,192},{65,1},{129,65},{193,129},{1,193... | collective-permute-start | bytes 442376 | tf_op jit(solution)/shard_map/ppermute | solution.py:542
  12.5 6.8 %collective-permute-start.3 = (bf16[576,128]{1,0:T(8,128)(2,1)S(1)}, bf16[576,128]{1,0:T(8,128)(2,1)S(1)}, u32[]{:S(2)}, u32[]{:S(2)}) collective-permute-start(bf16[576,128]{1,0:T(8,128)(2,1)S(1)} %get-tuple-element.16), channel_id=1, source_target_pairs={{192,0},{0,64},{64,128},{128,192},{193,1},{1,65},{65,129},{129,193... | collective-permute-start | bytes 442376 | tf_op jit(solution)/shard_map/ppermute | solution.py:542
  12.5 4.8 %collective-permute-start = (bf16[16,3072]{1,0:T(8,128)(2,1)S(1)}, bf16[16,3072]{1,0:T(8,128)(2,1)S(1)}, u32[]{:S(2)}, u32[]{:S(2)}) collective-permute-start(bf16[16,3072]{1,0:T(8,128)(2,1)S(1)} %get-tuple-element.13), channel_id=1, source_target_pairs={{4,0},{8,4},{12,8},{16,12},{20,16},{24,20},{28,24},{32,28},{36,32}... | collective-permute-start | bytes 294920 | tf_op jit(solution)/shard_map/ppermute | solution.py:542
  14.4 4.8 %collective-permute-start.1 = (bf16[16,3072]{1,0:T(8,128)(2,1)S(1)}, bf16[16,3072]{1,0:T(8,128)(2,1)S(1)}, u32[]{:S(2)}, u32[]{:S(2)}) collective-permute-start(bf16[16,3072]{1,0:T(8,128)(2,1)S(1)} %get-tuple-element.14), channel_id=1, source_target_pairs={{60,0},{0,4},{4,8},{8,12},{12,16},{16,20},{20,24},{24,28},{28,32},... | collective-permute-start | bytes 294920 | tf_op jit(solution)/shard_map/ppermute | solution.py:542
  17.3 2.0 %copy-start.6 = (bf16[16,3072]{1,0:T(8,128)(2,1)}, bf16[16,3072]{1,0:T(8,128)(2,1)S(1)}, u32[]{:S(2)}) copy-start(bf16[16,3072]{1,0:T(8,128)(2,1)S(1)} %collective-permute-done.ra) | copy-start | bytes 294916
  19.3 0.6 copy-start.7
  19.3 0.7 copy-start.4
  19.3 0.7 copy-start.5

commit v2 on v1

v2 whole, which is shorter than its diff:
```python
import functools
import math

import jax
import jax.numpy as jnp
import ml_dtypes
import numpy as np
from jax import lax
from jax.experimental import pallas as pl
from jax.experimental.pallas import tpu as pltpu
from jax.sharding import PartitionSpec as P

MESH = pl.DeviceIdType.MESH
BF = jnp.bfloat16
F32 = jnp.float32
T = 90
C = 32
SL = 6
G = 96
R = SL * G
W = T * C
WP = 3072
NB = 12
LAST = W - 11 * 256
VMEM_LIMIT = 60 * 2**20
XW = WP + 256


def spread_matrix():
    m = np.zeros((256, WP), np.float32)
    for j in range(T):
        m[j, j * C : (j + 1) * C] = 1
        m[128 + j, j * C : (j + 1) * C] = 1
    return m.astype(ml_dtypes.bfloat16)


def flip_lanes_matrix():
    m = np.zeros((256, 128), np.float32)
    for q in range(4):
        for k in range(C):
            m[C * (5 - q) + k, C * q + k] = 1
    return m.astype(ml_dtypes.bfloat16)


def flip_rows_matrix():
    m = np.zeros((G, G), np.float32)
    for i in range(T):
        m[i, T - 1 - i] = 1
    return m.astype(ml_dtypes.bfloat16)


def dot(a, b):
    return jnp.dot(a, b, preferred_element_type=F32)


def dot_t(a, b):
    return lax.dot_general(a, b, (((1,), (1,)), ((), ())), preferred_element_type=F32)


def split_hi_lo(v):
    hi = v.astype(BF)
    lo = (v - hi.astype(F32)).astype(BF)
    return hi, lo


def device_kernel(
    sizes,
    nb,
    rev,
    x_hbm,
    g_hbm,
    wa,
    spread,
    flip_l,
    flip_r,
    weight_t,
    bias,
    y_hbm,
    gi_hbm,
    w_out,
    b_out,
    xs,
    gs,
    x1,
    s3,
    xp,
    wet,
    cols,
    row_out,
    row_in,
    col_out,
    col_in,
    rim,
    gacc,
    part,
    got1,
    mine,
    got2,
    full,
    in_sem,
    out_sem,
    halo_s,
    halo_r,
    s_sem1,
    r_sem1,
    s_sem2,
    r_sem2,
    s_sem3,
    r_sem3,
):
    n_face, n_tile, n_dp, scale = sizes
    f, t, d = lax.axis_index("face"), lax.axis_index("tile"), lax.axis_index("dp")
    n_plane = n_face * n_dp
    me = f * n_dp + d

    def tile_peer(k):
        return (f, lax.rem(t + k, n_tile), d)

    def face_peer(k):
        return (lax.rem(f + k, n_face), t, d)

    def plane_peer(k):
        q = lax.rem(me + k, n_plane)
        return (q // n_dp, t, lax.rem(q, n_dp))

    copies = []
    for s in range(SL):
        copies.append(pltpu.make_async_copy(x_hbm.at[0, s], xs.at[s], in_sem.at[0, s]))
        copies.append(pltpu.make_async_copy(g_hbm.at[0, s], gs.at[s], in_sem.at[1, s]))
    for copy in copies:
        copy.start()

    barrier = pltpu.get_barrier_semaphore()
    for k in range(1, n_tile):
        pl.semaphore_signal(barrier, inc=1, device_id=tile_peer(k), device_id_type=MESH)
    for k in range(1, n_plane):
        pl.semaphore_signal(barrier, inc=1, device_id=plane_peer(k), device_id_type=MESH)

    area = []
    for s in range(SL):
        v = jnp.concatenate([wa[s], jnp.zeros((G - T, T), F32)], 0)
        area.append(jnp.concatenate([v, jnp.zeros((G, 128 - T), F32)], 1))
    hi, lo = split_hi_lo(jnp.concatenate(area, 0))
    area = jnp.concatenate([hi, lo], 1)

    w = weight_t[...].astype(F32)
    w = jnp.concatenate([w, jnp.zeros((C, 96), F32)], 1).T[0 : 9 * C]

    def tap(a, c):
        start = (3 * a + c) * C
        return w[start : start + C]

    def band(a, cells_in, shift, mirror=False):
        rows_iota = lax.broadcasted_iota(jnp.int32, (256, cells_in * C), 0) // C
        lanes_iota = lax.broadcasted_iota(jnp.int32, (256, cells_in * C), 1) // C - shift
        which = rows_iota - lanes_iota + 1
        if mirror:
            which = 2 - which
        out = jnp.zeros((256, cells_in * C), F32)
        for c in range(3):
            wide = jnp.concatenate([tap(a, c)] * 4, 1)
            wide = jnp.concatenate([wide] * (cells_in // 4), 1)
            out = jnp.where(which == c, jnp.concatenate([wide] * 8, 0), out)
        return out.astype(BF)

    bands = [band(a, 8, 0) for a in range(3)]
    z32 = jnp.zeros((C, C), F32)
    z64 = jnp.zeros((C, 192), F32)
    wq_rows = []
    for a in range(3):
        wq_rows.append(jnp.concatenate([tap(a, 0), z32, z64], 1))
        wq_rows.append(jnp.concatenate([z64, z32, tap(a, 2)], 1))
    wq = jnp.concatenate(wq_rows + [jnp.zeros((64, 256), F32)], 0).astype(BF)
    gl = jnp.concatenate([v for a in range(3) for v in (tap(2 - a, 2), z32)] + [z32, z32], 1)
    gr = jnp.concatenate([v for a in range(3) for v in (z32, tap(2 - a, 0))] + [z32, z32], 1)
    wqb = jnp.concatenate([gl, jnp.zeros((192, 256), F32), gr], 0).astype(BF)

    for copy in copies:
        copy.wait()

    zrow = jnp.zeros((2, 256), BF)
    for side, row in ((0, 0), (1, T - 1)):
        lhs = jnp.concatenate([area[G * s + row : G * s + row + 1] for s in range(SL)] + [zrow], 0)
        wide = dot(lhs, spread[...])
        for place, ref in ((0, xs), (8, gs)):
            v = [ref[s, row : row + 1, :].astype(F32) for s in range(SL)]
            v = jnp.concatenate(v + [jnp.zeros((2, W), F32)], 0)
            v = jnp.concatenate([v, jnp.zeros((8, WP - W), F32)], 1)
            v = v * wide if place else v
            v = jnp.where(wide > 0, v, 0.0)
            if place == 0:
                kept = v
            else:
                row_out[side] = jnp.concatenate([kept, v], 0).astype(BF)
    pad = jnp.zeros((G - T, 128), BF)
    for side, col in ((0, 0), (1, T - 1)):
        for s in range(SL):
            e = jnp.broadcast_to(wa[s, :, col : col + 1], (T, C))
            xv = jnp.where(e > 0, xs[s, :, C * col : C * col + C].astype(F32), 0.0)
            gv = jnp.where(e > 0, e * gs[s, :, C * col : C * col + C].astype(F32), 0.0)
            v = jnp.concatenate([xv, gv, jnp.zeros((T, 64), F32)], 1).astype(BF)
            col_out[side, s * G : (s + 1) * G] = jnp.concatenate([v, pad], 0)

    pl.semaphore_wait(barrier, n_tile + n_plane - 2)
    halo = []
    for src, dst, k, target in (
        (row_out.at[1], row_in.at[0], 0, tile_peer(n_tile - 1)),
        (row_out.at[0], row_in.at[1], 1, tile_peer(1)),
        (col_out.at[0], col_in.at[0], 2, face_peer(n_face - 1)),
        (col_out.at[1], col_in.at[1], 3, face_peer(1)),
    ):
        copy = pltpu.make_async_remote_copy(
            src_ref=src,
            dst_ref=dst,
            send_sem=halo_s.at[k],
            recv_sem=halo_r.at[k],
            device_id=target,
            device_id_type=MESH,
        )
        copy.start()
        halo.append(copy)

    def fetch(ref, m, lanes):
        parts = []
        for s in range(SL):
            start = 256 * m if isinstance(m, int) else pl.multiple_of(256 * m, 256)
            v = ref[s, :, pl.ds(start, lanes)].astype(F32)
            if lanes < 256:
                v = jnp.concatenate([v, jnp.zeros((T, 256 - lanes), F32)], 1)
            parts.append(v)
            parts.append(jnp.zeros((G - T, 256), F32))
        return jnp.concatenate(parts, 0)

    def down(v):
        return jnp.concatenate([v[R - 1 :], v[: R - 1]], 0)

    def up(v):
        return jnp.concatenate([v[1:], v[:1]], 0)

    def at(base, size, unit=128):
        return pl.ds(base if isinstance(base, int) else pl.multiple_of(base, unit), size)

    def blocks(body, first=True):
        if first:
            body(0, 256)
        else:
            pass
        lax.fori_loop(1 if first else 0, NB - 1, lambda m, c: (body(m, 256), c)[1], 0)
        body(NB - 1, LAST)

    zcol = jnp.zeros((R, 128), BF)
    for a in range(3):
        s3[a, :, 0:128] = zcol
        s3[a, :, XW - 128 : XW] = zcol
    x1[:, XW - 128 : XW] = zcol
    gacc[0:8] = jnp.zeros((8, 256), F32)

    def prepare(m, lanes):
        e = dot(area, spread[:, at(256 * m, 256)])
        blk = at(256 * m + 128, 256)
        wet[:, at(256 * m, 256)] = (e > 0).astype(F32).astype(BF)
        x1[:, blk] = jnp.where(e > 0, fetch(xs, m, lanes), 0.0).astype(BF)
        sv = jnp.where(e > 0, e * fetch(gs, m, lanes), 0.0).astype(BF)
        s3[0, :, blk] = down(sv)
        s3[1, :, blk] = sv
        s3[2, :, blk] = up(sv)
        gacc[0:8] = gacc[0:8] + jnp.sum(sv.astype(F32).reshape(R // 8, 8, 256), 0)

    blocks(prepare, first=False)
    row = jnp.sum(gacc[0:8], 0, keepdims=True)
    row = row[:, 0:128] + row[:, 128:256]
    row = row[:, 0:64] + row[:, 64:128]
    row = row[:, 0:C] + row[:, C : 2 * C]
    low = jnp.concatenate([row, jnp.zeros((1, 96), F32)], 1)
    part[96:128] = jnp.concatenate([low, jnp.zeros((31, 128), F32)], 0)

    for copy in halo:
        copy.wait()

    zr = jnp.concatenate([row_in[0], row_in[1]], 0)
    zpad = jnp.concatenate([jnp.zeros((32, 128), BF), zr], 1)
    stacked = jnp.concatenate([zpad[:, 128 * (22 - n) : 128 * (24 - n)] for n in range(23)], 0)
    turned = dot(stacked, flip_l[...]).astype(BF)
    flipped = jnp.concatenate(
        [turned[32 * n : 32 * n + 32] for n in range(23)] + [jnp.zeros((32, 128), BF)], 1
    )
    lane_i = lax.broadcasted_iota(jnp.int32, (128, 64), 1)
    row_i = lax.broadcasted_iota(jnp.int32, (128, 64), 0)
    sel = jnp.zeros((128, 64), F32)
    for s in range(SL):
        for side, halo_row in ((0, (16 * (s - 1) + 15) % 96), (1, 16 * s + 10)):
            n, r = nb[side, s], rev[side, s]
            src = 16 * side + 32 * r + lax.rem(jnp.maximum(n, 0), SL)
            src = jnp.where(n >= 0, src, -100)
            sel = jnp.where((row_i == halo_row) & (lane_i == src), 1.0, sel)
            rim_row = 96 + 16 * side + 8 * r + s
            sel = jnp.where((row_i == rim_row) & (lane_i == src + 8), 1.0, sel)
    routed = dot(sel.astype(BF), jnp.concatenate([zr, flipped], 0))
    for s in range(SL):
        rows = slice(G * s + 80, G * s + 96)
        old = x1[rows, 128 : 128 + WP].astype(F32)
        x1[rows, 128 : 128 + WP] = (old + routed[16 * s : 16 * s + 16]).astype(BF)
    hs = routed[96:128]
    hs = jnp.concatenate([jnp.zeros((32, 128), F32), hs, jnp.zeros((32, 128), F32)], 1)
    for side, a in ((0, 2), (1, 0)):
        total = None
        for r in range(2):
            rows = hs[16 * side + 8 * r : 16 * side + 8 * r + 8]
            lhs = jnp.concatenate(
                [rows[:, 256 * m : 256 * m + 512] for m in range(NB)], 0
            ).astype(BF)
            part_sum = dot_t(lhs, band(a, 16, 4, mirror=(r == 1)))
            total = part_sum if total is None else total + part_sum
        rim[side] = total.astype(BF).astype(F32)

    for side in range(2):
        flat = jnp.concatenate([col_in[side, s * G : (s + 1) * G] for s in range(SL)], 1)
        back = dot(flip_r[...], flat)
        for s in range(SL):
            cols[side, 0, s] = col_in[side, s * G : (s + 1) * G].astype(F32)
            cols[side, 1, s] = back[:, 128 * s : 128 * s + 128]
    ecol, xleft, xright = [], [], []
    for s in range(SL):
        got = []
        pieces = []
        for side in range(2):
            n, r = nb[2 + side, s], rev[2 + side, s]
            v = cols[side, r, lax.rem(jnp.maximum(n, 0), SL)]
            v = jnp.where(n >= 0, v, 0.0)
            got.append(v)
            pieces.append(jnp.where(r == 0, v, 0.0)[:, C : 2 * C])
            pieces.append(jnp.where(r == 1, v, 0.0)[:, C : 2 * C])
        ecol.append(jnp.concatenate(pieces, 1))
        xright.append(got[0][:, 0:C])
        xleft.append(got[1][:, 0:C])
    ecol = jnp.concatenate(ecol, 0)
    xright = jnp.concatenate(xright, 0)
    xleft = jnp.concatenate(xleft, 0)
    e3 = jnp.concatenate(
        [pltpu.roll(ecol, 1, 0), ecol, pltpu.roll(ecol, R - 1, 0)], 1
    ).astype(BF)
    v2 = jnp.concatenate(
        [v for a in range(3) for v in (tap(2 - a, 0), tap(a, 0), z32, z32)], 1
    )
    v3 = jnp.concatenate(
        [v for a in range(3) for v in (z32, z32, tap(2 - a, 2), tap(a, 2))], 1
    )
    rim_col = dot_t(e3, jnp.concatenate([v2, v3], 0).astype(BF)).astype(BF).astype(F32)
    zc = jnp.zeros((R, C), F32)
    x1[:, 0:128] = jnp.concatenate([zc, zc, zc, xleft], 1).astype(BF)
    right = at(128 + 128 * 22, 128)
    x1[:, right] = (
        x1[:, right].astype(F32) + jnp.concatenate([zc, zc, xright, zc], 1)
    ).astype(BF)

    def move(n, c):
        left = x1[:, at(128 * n, 128)][:, 96:128]
        xp[:, at(128 * n, 128)] = jnp.concatenate(
            [left, x1[:, at(128 * n + 128, 128)][:, 0:96]], 1
        )
        return c

    lax.fori_loop(0, 24, move, 0)

    gacc[...] = jnp.zeros_like(gacc)

    def outer(m, c):
        sv = jnp.concatenate([s3[2 - a, :, at(128 * m + 128, 128)] for a in range(3)], 1)
        gacc[...] += lax.dot_general(
            sv, xp[:, at(128 * m, 256)], (((0,), (0,)), ((), ())), preferred_element_type=F32
        )
        return c

    lax.fori_loop(0, 23, outer, 0)
    grad = gacc[...]
    for a in range(3):
        total = None
        for j in range(4):
            piece = grad[128 * a + C * j : 128 * a + C * j + C, C * j : C * j + 96]
            total = piece if total is None else total + piece
        part[C * a : C * a + C] = jnp.concatenate([total, jnp.zeros((C, C), F32)], 1)

    def rows8(i):
        return pl.ds(pl.multiple_of(i * 8, 8), 8)

    sends = []
    for k in range(1, n_tile):
        copy = pltpu.make_async_remote_copy(
            src_ref=part.at[rows8(lax.rem(t + k, n_tile))],
            dst_ref=got1.at[k],
            send_sem=s_sem1.at[k],
            recv_sem=r_sem1.at[k],
            device_id=tile_peer(k),
            device_id_type=MESH,
        )
        copy.start()
        sends.append(copy)

    def beside(ref, m):
        mid = ref[:, at(256 * m, 128)][:, 96:128]
        far = ref[:, at(256 * m + 384, 128)][:, 0:C]
        q = jnp.concatenate([mid, far, mid, far], 1)
        lane = lax.broadcasted_iota(jnp.int32, (R, 128), 1)
        return jnp.concatenate([jnp.where(lane < 64, down(q), q), up(q)], 1)

    bias_row = jnp.concatenate([bias[...]] * 8, 1)

    def forward(m, lanes):
        xv = x1[:, at(256 * m + 128, 256)]
        y = dot(down(xv), bands[0]) + dot(xv, bands[1])
        y = y + dot(up(xv), bands[2]) + dot(beside(x1, m), wq) + bias_row
        y = (y * wet[:, at(256 * m, 256)].astype(F32)).astype(BF)
        for s in range(SL):
            xs[s, :, at(256 * m, lanes)] = y[G * s : G * s + T, :lanes]

    blocks(forward, first=False)
    out_copies = []
    for s in range(SL):
        out_copies.append(pltpu.make_async_copy(xs.at[s], y_hbm.at[0, s], out_sem.at[0, s]))
        out_copies[-1].start()

    for copy in sends:
        copy.wait()
    total = part[rows8(t)]
    for k in range(1, n_tile):
        total = total + got1[k]
    mine[...] = total
    sends = []
    for k in range(1, n_plane):
        copy = pltpu.make_async_remote_copy(
            src_ref=mine,
            dst_ref=got2.at[me],
            send_sem=s_sem2.at[k],
            recv_sem=r_sem2.at[k],
            device_id=plane_peer(k),
            device_id_type=MESH,
        )
        copy.start()
        sends.append(copy)
    got2[me] = total

    row8 = lax.broadcasted_iota(jnp.int32, (8, 256), 0)
    z6 = jnp.zeros((R, 192), F32)

    def backward(m, lanes):
        blk = at(256 * m + 128, 256)
        y = dot_t(s3[0, :, blk], bands[2]) + dot_t(s3[1, :, blk], bands[1])
        y = y + dot_t(s3[2, :, blk], bands[0]) + dot_t(beside(s3.at[1], m), wqb)
        if isinstance(m, int) and m == 0:
            y = y + jnp.concatenate([rim_col[:, C : 2 * C], zc, z6], 1)
        if isinstance(m, int) and m == NB - 1:
            y = y + jnp.concatenate([zc, rim_col[:, 0:C], z6], 1)
        parts = []
        tops = rim[0, at(8 * m, 8, 8), :]
        lows = rim[1, at(8 * m, 8, 8), :]
        for s in range(SL):
            parts.append(y[G * s : G * s + 8] + jnp.where(row8 == 0, tops[s : s + 1], 0.0))
            parts.append(y[G * s + 8 : G * s + 88])
            parts.append(y[G * s + 88 : G * s + 96] + jnp.where(row8 == 1, lows[s : s + 1], 0.0))
        y = jnp.concatenate(parts, 0)
        y = (y * wet[:, at(256 * m, 256)].astype(F32)).astype(BF)
        for s in range(SL):
            gs[s, :, at(256 * m, lanes)] = y[G * s : G * s + T, :lanes]

    backward(0, 256)
    lax.fori_loop(1, 6, lambda m, c: (backward(m, 256), c)[1], 0)

    for copy in sends:
        copy.wait()
    total = got2[0]
    for k in range(1, n_plane):
        total = total + got2[k]
    full[rows8(t)] = total * scale
    sends = []
    for k in range(1, n_tile):
        copy = pltpu.make_async_remote_copy(
            src_ref=full.at[rows8(t)],
            dst_ref=full.at[rows8(t)],
            send_sem=s_sem3.at[k],
            recv_sem=r_sem3.at[k],
            device_id=tile_peer(k),
            device_id_type=MESH,
        )
        copy.start()
        sends.append(copy)

    lax.fori_loop(6, NB - 1, lambda m, c: (backward(m, 256), c)[1], 0)
    backward(NB - 1, LAST)
    for s in range(SL):
        out_copies.append(pltpu.make_async_copy(gs.at[s], gi_hbm.at[0, s], out_sem.at[1, s]))
        out_copies[-1].start()

    for copy in sends:
        copy.wait()
    for a in range(3):
        w_out[a] = full[C * a : C * a + C]
    b_out[...] = full[96:97, 0:C]
    for copy in out_copies:
        copy.wait()


def per_device(
    inputs, cotangent, conv_weight, out_bias, cell_area, land_mask, neighbours, reversal, wet_count
):
    occupied = jnp.arange(SL, dtype=jnp.int32) < wet_count[0]
    wa = jnp.where((land_mask != 0) & occupied[:, None], cell_area, 0.0).reshape(SL, T, T)
    n_face, n_tile, n_dp = (lax.axis_size(a) for a in ("face", "tile", "dp"))
    n_plane = n_face * n_dp
    scale = 1.0 / math.sqrt(n_dp * n_face * n_tile * SL * T * T)
    any_ = pl.BlockSpec(memory_space=pl.ANY)
    vm = pl.BlockSpec(memory_space=pltpu.VMEM)
    sm = pl.BlockSpec(memory_space=pltpu.SMEM)
    tiles = jax.ShapeDtypeStruct((1, SL, T, W), BF)
    dma = pltpu.SemaphoreType.DMA
    outputs, input_grad, w_sum, b_sum = pl.pallas_call(
        functools.partial(device_kernel, (n_face, n_tile, n_dp, scale)),
        in_specs=[sm, sm, any_, any_] + [vm] * 6,
        out_specs=[any_, any_, vm, vm],
        out_shape=[
            tiles,
            tiles,
            jax.ShapeDtypeStruct((3, C, 128), F32),
            jax.ShapeDtypeStruct((1, C), F32),
        ],
        scratch_shapes=[
            pltpu.VMEM((SL, T, W), BF),
            pltpu.VMEM((SL, T, W), BF),
            pltpu.VMEM((R, XW), BF),
            pltpu.VMEM((3, R, XW), BF),
            pltpu.VMEM((R, WP), BF),
            pltpu.VMEM((R, WP), BF),
            pltpu.VMEM((2, 2, SL, G, 128), F32),
            pltpu.VMEM((2, 16, WP), BF),
            pltpu.VMEM((2, 16, WP), BF),
            pltpu.VMEM((2, R, 128), BF),
            pltpu.VMEM((2, R, 128), BF),
            pltpu.VMEM((2, 8 * NB, 256), F32),
            pltpu.VMEM((384, 256), F32),
            pltpu.VMEM((128, 128), F32),
            pltpu.VMEM((n_tile, 8, 128), F32),
            pltpu.VMEM((8, 128), F32),
            pltpu.VMEM((n_plane, 8, 128), F32),
            pltpu.VMEM((128, 128), F32),
            dma((2, SL)),
            dma((2, SL)),
            dma((4,)),
            dma((4,)),
            dma((n_tile,)),
            dma((n_tile,)),
            dma((n_plane,)),
            dma((n_plane,)),
            dma((n_tile,)),
            dma((n_tile,)),
        ],
        compiler_params=pltpu.CompilerParams(
            vmem_limit_bytes=VMEM_LIMIT, collective_id=0, has_side_effects=True
        ),
    )(
        neighbours.T,
        reversal.T,
        inputs,
        cotangent,
        wa,
        jnp.asarray(spread_matrix()),
        jnp.asarray(flip_lanes_matrix()),
        jnp.asarray(flip_rows_matrix()),
        conv_weight.T,
        out_bias[None],
    )
    weight_grad = w_sum[:, :, 0 : 3 * C].transpose(0, 2, 1).reshape(9 * C, C)
    return outputs, input_grad, weight_grad, b_sum[0]


def solution(mesh):
    return jax.shard_map(
        per_device,
        mesh=mesh,
        in_specs=(
            P("dp", ("face", "tile"), None, None),
            P("dp", ("face", "tile"), None, None),
            P(),
            P(),
            P(("face", "tile"), None),
            P(("face", "tile"), None),
            P(("face", "tile"), None),
            P(("face", "tile"), None),
            P(("face", "tile")),
        ),
        out_specs=(
            P("dp", ("face", "tile"), None, None),
            P("dp", ("face", "tile"), None, None),
            P(),
            P(),
        ),
        check_vma=False,
    )
```

time: 77.7 us -> 62.6 us (0.81)
  starting transfers between devices: 5.87 us -> 0 us
  Pallas kernels: 55.5 us -> 50.9 us
  local copies, waits for them, and re-layouts: 11.3 us -> 9.03 us
  waiting for transfers between devices: 2.19 us -> 0 us
    ppermute x4 -> x0, starting transfers between devices: 5.87 us -> none  [passed_along(): lax.ppermute(block, axis, [((i - distance) % n, i) for i in range(n)])]
    pallas_call x3 -> x1, Pallas kernels: 55.5 us -> 50.9 us  [per_device(): pl.pallas_call(functools.partial(device_kernel, (n_face, n_tile, n_dp, sc...]
    unnamed x27 -> x7, local copies, waits for them, and re-layouts: 10.9 us -> 6.35 us
    ppermute x4 -> x0, waiting for transfers between devices: 2.19 us -> none  [passed_along(): lax.ppermute(block, axis, [((i - distance) % n, i) for i in range(n)])]
    transpose x0 -> x2, local copies, waits for them, and re-layouts: none -> 0.84 us  [per_device(): weight_grad = w_sum[:, :, 0:3 * C].transpose(0, 2, 1).reshape(9 * C, C)]
  transfers between devices with their start and end apart: 4 -> 0, of which waited for: 2 -> 0; matrix products, arithmetic and copies ran while one was open for 3% -> 0% of each run, Pallas kernels for 0% -> 0%
where the time goes in v2:
time: 62.6 us; the launch traced here: 62.4 us
  Pallas kernels  50.9 us (81%)
  local copies, waits for them, and re-layouts  9.03 us (14%)
  between operations  1.3 us (2%)
  other arithmetic  1.14 us (2%)
    pallas_call x1, Pallas kernels, per_device(): pl.pallas_call(functools.partial(device_kernel, (n_face, n_tile, n_dp, sc...  50.9 us
    unnamed x7, local copies, waits for them, and re-layouts  6.35 us

profile of v2, /device:TPU:1, one launch (start us, length us, event | category | flops | bytes accessed | tf_op | source)
XLA Modules:
  0.0 62.4 jit_solution(3672332858606067205)
XLA Ops:
  1.3 1.1 %and_select_fusion = f32[6,8100]{1,0:T(8,128)S(1)} fusion(f32[6,8100]{1,0:T(8,128)} %param.16, s32[6,8100]{1,0:T(8,128)} %param.17, pred[6]{0:T(512)(128)(4,1)S(1)} %iota_compare_fusion), kind=kLoop, calls=%fused_computation | loop fusion | flops 145800 | bytes 583206 | tf_op jit(solution)/shard_map/jit(_where)/select_n | solution.py:506
  2.4 1.1 %reshape.18.wa = f32[6,90,90]{2,1,0:T(8,128)} reshape(f32[6,8100]{1,0:T(8,128)S(1)} %and_select_fusion) | data formatting | bytes 388800 | tf_op jit(solution)/shard_map/reshape | solution.py:506
  3.5 50.9 %shard_map.147 = (bf16[1,6,90,2880]{3,2,1,0:T(8,128)(2,1)}, bf16[1,6,90,2880]{3,2,1,0:T(8,128)(2,1)}, f32[3,32,128]{2,1,0:T(8,128)}, f32[1,32]{1,0:T(1,128)}) custom-call(s32[4,6]{1,0:T(4,128)} %bitcast.12, s32[4,6]{1,0:T(4,128)} %bitcast.13, bf16[1,6,90,2880]{3,2,1,0:T(8,128)(2,1)} %x_hbm.1, bf16[1,6,90,2880]{3,2,1,0:T(8,128)(2,1)} %g_hbm.1, ...), custom_call_target="tpu_custom_call" | custom-call | tf_op jit(solution)/shard_map/pallas_call | solution.py:515
  54.4 0.8 %slice_bitcast_fusion = f32[3,96,32]{1,2,0:T(8,128)S(1)} fusion(f32[3,32,128]{2,1,0:T(8,128)} %get-tuple-element.10), kind=kLoop, calls=%fused_computation.1 | loop fusion | bytes 73728 | tf_op jit(solution)/shard_map/transpose | solution.py:570
  55.3 0.7 %reshape.19 = f32[288,32]{0,1:T(8,128)} reshape(f32[3,96,32]{1,0,2:T(4,128)S(1)} %copy.16) | data formatting | bytes 73728 | tf_op jit(solution)/shard_map/reshape | solution.py:570
  56.0 0.0 copy-start
  56.0 4.1 %copy.21 = bf16[1,6,90,2880]{3,2,1,0:T(8,128)(2,1)} copy(bf16[1,6,90,2880]{3,2,1,0:T(8,128)(2,1)} %get-tuple-element.16) | data formatting | bytes 6220800
  60.1 0.0 copy-done
  60.1 0.0 copy-start.1
  60.1 1.7 %copy.22 = bf16[1,6,90,2880]{3,2,1,0:T(8,128)(2,1)} copy(bf16[1,6,90,2880]{3,2,1,0:T(8,128)(2,1)S(1)} %copy-done) | data formatting | bytes 6220800
  61.8 0.0 copy-done.1
  61.8 0.5 copy.23
  (2 shorter events, 0.0 us)
Async XLA Ops:
  56.0 4.1 %copy-start = (bf16[1,6,90,2880]{3,2,1,0:T(8,128)(2,1)S(1)}, bf16[1,6,90,2880]{3,2,1,0:T(8,128)(2,1)}, u32[]{:S(2)}) copy-start(bf16[1,6,90,2880]{3,2,1,0:T(8,128)(2,1)} %get-tuple-element.17) | copy-start | bytes 9331204
  60.1 1.7 %copy-start.1 = (f32[1,32]{1,0:T(1,128)S(1)}, f32[1,32]{1,0:T(1,128)}, u32[]{:S(2)}) copy-start(f32[1,32]{1,0:T(1,128)} %get-tuple-element.11) | copy-start | bytes 388

commit v3 on v2

--- a/solution.py
+++ b/solution.py
@@ -3,8 +3,6 @@
 
 import jax
 import jax.numpy as jnp
-import ml_dtypes
-import numpy as np
 from jax import lax
 from jax.experimental import pallas as pl
 from jax.experimental.pallas import tpu as pltpu
@@ -26,29 +24,6 @@
 XW = WP + 256
 
 
-def spread_matrix():
-    m = np.zeros((256, WP), np.float32)
-    for j in range(T):
-        m[j, j * C : (j + 1) * C] = 1
-        m[128 + j, j * C : (j + 1) * C] = 1
-    return m.astype(ml_dtypes.bfloat16)
-
-
-def flip_lanes_matrix():
-    m = np.zeros((256, 128), np.float32)
-    for q in range(4):
-        for k in range(C):
-            m[C * (5 - q) + k, C * q + k] = 1
-    return m.astype(ml_dtypes.bfloat16)
-
-
-def flip_rows_matrix():
-    m = np.zeros((G, G), np.float32)
-    for i in range(T):
-        m[i, T - 1 - i] = 1
-    return m.astype(ml_dtypes.bfloat16)
-
-
 def dot(a, b):
     return jnp.dot(a, b, preferred_element_type=F32)
 
@@ -69,10 +44,9 @@
     rev,
     x_hbm,
     g_hbm,
-    wa,
-    spread,
-    flip_l,
-    flip_r,
+    count,
+    area_in,
+    mask_in,
     weight_t,
     bias,
     y_hbm,
@@ -81,7 +55,15 @@
     b_out,
     xs,
     gs,
-    x1,
+    spread,
+    by_row,
+    area_ref,
+    bands,
+    wq,
+    wqb,
+    rim_col,
+    hs_ref,
+    x3,
     s3,
     xp,
     wet,
@@ -136,13 +118,6 @@
     for k in range(1, n_plane):
         pl.semaphore_signal(barrier, inc=1, device_id=plane_peer(k), device_id_type=MESH)
 
-    area = []
-    for s in range(SL):
-        v = jnp.concatenate([wa[s], jnp.zeros((G - T, T), F32)], 0)
-        area.append(jnp.concatenate([v, jnp.zeros((G, 128 - T), F32)], 1))
-    hi, lo = split_hi_lo(jnp.concatenate(area, 0))
-    area = jnp.concatenate([hi, lo], 1)
-
     w = weight_t[...].astype(F32)
     w = jnp.concatenate([w, jnp.zeros((C, 96), F32)], 1).T[0 : 9 * C]
 
@@ -163,43 +138,65 @@
             out = jnp.where(which == c, jnp.concatenate([wide] * 8, 0), out)
         return out.astype(BF)
 
-    bands = [band(a, 8, 0) for a in range(3)]
-    z32 = jnp.zeros((C, C), F32)
-    z64 = jnp.zeros((C, 192), F32)
-    wq_rows = []
-    for a in range(3):
-        wq_rows.append(jnp.concatenate([tap(a, 0), z32, z64], 1))
-        wq_rows.append(jnp.concatenate([z64, z32, tap(a, 2)], 1))
-    wq = jnp.concatenate(wq_rows + [jnp.zeros((64, 256), F32)], 0).astype(BF)
-    gl = jnp.concatenate([v for a in range(3) for v in (tap(2 - a, 2), z32)] + [z32, z32], 1)
-    gr = jnp.concatenate([v for a in range(3) for v in (z32, tap(2 - a, 0))] + [z32, z32], 1)
-    wqb = jnp.concatenate([gl, jnp.zeros((192, 256), F32), gr], 0).astype(BF)
+    @pl.when(t >= 0)
+    def _():
+        slot_i = lax.broadcasted_iota(jnp.int32, (SL, T * T), 0)
+        flat = jnp.where((mask_in[...] != 0) & (slot_i < count[0]), area_in[...], 0.0)
+        flat = jnp.concatenate([flat, jnp.zeros((2, T * T), F32)], 0)
+        for i in range(T):
+            by_row[i] = jnp.concatenate([flat[:, T * i : T * i + T], jnp.zeros((8, 128 - T), F32)], 1)
+        by_row[T:G] = jnp.zeros((G - T, 8, 128), F32)
+        wa = [by_row[:, s, :] for s in range(SL)]
+        hi, lo = split_hi_lo(jnp.concatenate(wa, 0))
+        area_ref[...] = jnp.concatenate([hi, lo], 1)
+
+        for m in range(NB):
+            r_i = lax.broadcasted_iota(jnp.int32, (256, 256), 0)
+            l_i = lax.broadcasted_iota(jnp.int32, (256, 256), 1)
+            hit = (r_i & 127) == (l_i >> 5) + 8 * m
+            spread[:, 256 * m : 256 * m + 256] = jnp.where(hit & ((r_i & 127) < T), 1.0, 0.0).astype(BF)
+
+        for a in range(3):
+            bands[a] = band(a, 8, 0)
+        z32 = jnp.zeros((C, C), F32)
+        z64 = jnp.zeros((C, 192), F32)
+        wq_rows = []
+        for a in range(3):
+            wq_rows.append(jnp.concatenate([tap(a, 0), z32, z64], 1))
+            wq_rows.append(jnp.concatenate([z64, z32, tap(a, 2)], 1))
+        wq[...] = jnp.concatenate(wq_rows + [jnp.zeros((64, 256), F32)], 0).astype(BF)
+        gl = jnp.concatenate([v for a in range(3) for v in (tap(2 - a, 2), z32)] + [z32, z32], 1)
+        gr = jnp.concatenate([v for a in range(3) for v in (z32, tap(2 - a, 0))] + [z32, z32], 1)
+        wqb[...] = jnp.concatenate([gl, jnp.zeros((192, 256), F32), gr], 0).astype(BF)
 
     for copy in copies:
         copy.wait()
 
-    zrow = jnp.zeros((2, 256), BF)
-    for side, row in ((0, 0), (1, T - 1)):
-        lhs = jnp.concatenate([area[G * s + row : G * s + row + 1] for s in range(SL)] + [zrow], 0)
-        wide = dot(lhs, spread[...])
-        for place, ref in ((0, xs), (8, gs)):
-            v = [ref[s, row : row + 1, :].astype(F32) for s in range(SL)]
-            v = jnp.concatenate(v + [jnp.zeros((2, W), F32)], 0)
-            v = jnp.concatenate([v, jnp.zeros((8, WP - W), F32)], 1)
-            v = v * wide if place else v
-            v = jnp.where(wide > 0, v, 0.0)
-            if place == 0:
-                kept = v
-            else:
-                row_out[side] = jnp.concatenate([kept, v], 0).astype(BF)
-    pad = jnp.zeros((G - T, 128), BF)
-    for side, col in ((0, 0), (1, T - 1)):
-        for s in range(SL):
-            e = jnp.broadcast_to(wa[s, :, col : col + 1], (T, C))
-            xv = jnp.where(e > 0, xs[s, :, C * col : C * col + C].astype(F32), 0.0)
-            gv = jnp.where(e > 0, e * gs[s, :, C * col : C * col + C].astype(F32), 0.0)
-            v = jnp.concatenate([xv, gv, jnp.zeros((T, 64), F32)], 1).astype(BF)
-            col_out[side, s * G : (s + 1) * G] = jnp.concatenate([v, pad], 0)
+    @pl.when(t >= 0)
+    def _():
+        wa = [by_row[:, s, :] for s in range(SL)]
+        for side, row in ((0, 0), (1, T - 1)):
+            lhs = [by_row[row, s : s + 1, :] for s in range(SL)] + [jnp.zeros((2, 128), F32)]
+            lhs = jnp.concatenate(split_hi_lo(jnp.concatenate(lhs, 0)), 1)
+            wide = dot(lhs, spread[...])
+            for place, ref in ((0, xs), (8, gs)):
+                v = [ref[s, row : row + 1, :].astype(F32) for s in range(SL)]
+                v = jnp.concatenate(v + [jnp.zeros((2, W), F32)], 0)
+                v = jnp.concatenate([v, jnp.zeros((8, WP - W), F32)], 1)
+                v = v * wide if place else v
+                v = jnp.where(wide > 0, v, 0.0)
+                if place == 0:
+                    kept = v
+                else:
+                    row_out[side] = jnp.concatenate([kept, v], 0).astype(BF)
+        pad = jnp.zeros((G - T, 128), BF)
+        for side, col in ((0, 0), (1, T - 1)):
+            for s in range(SL):
+                e = jnp.broadcast_to(wa[s][0:T, col : col + 1], (T, C))
+                xv = jnp.where(e > 0, xs[s, :, C * col : C * col + C].astype(F32), 0.0)
+                gv = jnp.where(e > 0, e * gs[s, :, C * col : C * col + C].astype(F32), 0.0)
+                v = jnp.concatenate([xv, gv, jnp.zeros((T, 64), F32)], 1).astype(BF)
+                col_out[side, s * G : (s + 1) * G] = jnp.concatenate([v, pad], 0)
 
     pl.semaphore_wait(barrier, n_tile + n_plane - 2)
     halo = []
@@ -240,47 +237,52 @@
     def at(base, size, unit=128):
         return pl.ds(base if isinstance(base, int) else pl.multiple_of(base, unit), size)
 
-    def blocks(body, first=True):
-        if first:
-            body(0, 256)
-        else:
-            pass
-        lax.fori_loop(1 if first else 0, NB - 1, lambda m, c: (body(m, 256), c)[1], 0)
-        body(NB - 1, LAST)
-
-    zcol = jnp.zeros((R, 128), BF)
-    for a in range(3):
-        s3[a, :, 0:128] = zcol
-        s3[a, :, XW - 128 : XW] = zcol
-    x1[:, XW - 128 : XW] = zcol
-    gacc[0:8] = jnp.zeros((8, 256), F32)
-
-    def prepare(m, lanes):
-        e = dot(area, spread[:, at(256 * m, 256)])
-        blk = at(256 * m + 128, 256)
-        wet[:, at(256 * m, 256)] = (e > 0).astype(F32).astype(BF)
-        x1[:, blk] = jnp.where(e > 0, fetch(xs, m, lanes), 0.0).astype(BF)
-        sv = jnp.where(e > 0, e * fetch(gs, m, lanes), 0.0).astype(BF)
-        s3[0, :, blk] = down(sv)
-        s3[1, :, blk] = sv
-        s3[2, :, blk] = up(sv)
-        gacc[0:8] = gacc[0:8] + jnp.sum(sv.astype(F32).reshape(R // 8, 8, 256), 0)
-
-    blocks(prepare, first=False)
-    row = jnp.sum(gacc[0:8], 0, keepdims=True)
-    row = row[:, 0:128] + row[:, 128:256]
-    row = row[:, 0:64] + row[:, 64:128]
-    row = row[:, 0:C] + row[:, C : 2 * C]
-    low = jnp.concatenate([row, jnp.zeros((1, 96), F32)], 1)
-    part[96:128] = jnp.concatenate([low, jnp.zeros((31, 128), F32)], 0)
+    def blocks(body):
+        for m in range(NB):
+            body(m, 256 if m < NB - 1 else LAST)
+
+    x1 = x3.at[1]
+    @pl.when(t >= 0)
+    def _():
+        zcol = jnp.zeros((R, 128), BF)
+        for a in range(3):
+            s3[a, :, 0:128] = zcol
+            s3[a, :, XW - 128 : XW] = zcol
+        x1[:, XW - 128 : XW] = zcol
+        gacc[0:8] = jnp.zeros((8, 256), F32)
+
+        def prepare(m, lanes):
+            e = dot(area_ref[...], spread[:, at(256 * m, 256)])
+            blk = at(256 * m + 128, 256)
+            wet[:, at(256 * m, 256)] = (e > 0).astype(F32).astype(BF)
+            x1[:, blk] = jnp.where(e > 0, fetch(xs, m, lanes), 0.0).astype(BF)
+            sv = jnp.where(e > 0, e * fetch(gs, m, lanes), 0.0).astype(BF)
+            s3[0, :, blk] = down(sv)
+            s3[1, :, blk] = sv
+            s3[2, :, blk] = up(sv)
+            gacc[0:8] = gacc[0:8] + jnp.sum(sv.astype(F32).reshape(R // 8, 8, 256), 0)
+
+        blocks(prepare)
+        row = jnp.sum(gacc[0:8], 0, keepdims=True)
+        row = row[:, 0:128] + row[:, 128:256]
+        row = row[:, 0:64] + row[:, 64:128]
+        row = row[:, 0:C] + row[:, C : 2 * C]
+        low = jnp.concatenate([row, jnp.zeros((1, 96), F32)], 1)
+        part[96:128] = jnp.concatenate([low, jnp.zeros((31, 128), F32)], 0)
 
     for copy in halo:
         copy.wait()
 
+    r_i = lax.broadcasted_iota(jnp.int32, (256, 128), 0)
+    l_i = lax.broadcasted_iota(jnp.int32, (256, 128), 1)
+    flip_l = jnp.where(r_i == 160 - 32 * (l_i >> 5) + (l_i & 31), 1.0, 0.0).astype(BF)
+    r_i = lax.broadcasted_iota(jnp.int32, (G, G), 0)
+    l_i = lax.broadcasted_iota(jnp.int32, (G, G), 1)
+    flip_r = jnp.where(r_i + l_i == T - 1, 1.0, 0.0).astype(BF)
     zr = jnp.concatenate([row_in[0], row_in[1]], 0)
     zpad = jnp.concatenate([jnp.zeros((32, 128), BF), zr], 1)
     stacked = jnp.concatenate([zpad[:, 128 * (22 - n) : 128 * (24 - n)] for n in range(23)], 0)
-    turned = dot(stacked, flip_l[...]).astype(BF)
+    turned = dot(stacked, flip_l).astype(BF)
     flipped = jnp.concatenate(
         [turned[32 * n : 32 * n + 32] for n in range(23)] + [jnp.zeros((32, 128), BF)], 1
     )
@@ -301,21 +303,11 @@
         old = x1[rows, 128 : 128 + WP].astype(F32)
         x1[rows, 128 : 128 + WP] = (old + routed[16 * s : 16 * s + 16]).astype(BF)
     hs = routed[96:128]
-    hs = jnp.concatenate([jnp.zeros((32, 128), F32), hs, jnp.zeros((32, 128), F32)], 1)
-    for side, a in ((0, 2), (1, 0)):
-        total = None
-        for r in range(2):
-            rows = hs[16 * side + 8 * r : 16 * side + 8 * r + 8]
-            lhs = jnp.concatenate(
-                [rows[:, 256 * m : 256 * m + 512] for m in range(NB)], 0
-            ).astype(BF)
-            part_sum = dot_t(lhs, band(a, 16, 4, mirror=(r == 1)))
-            total = part_sum if total is None else total + part_sum
-        rim[side] = total.astype(BF).astype(F32)
+    hs_ref[...] = jnp.concatenate([jnp.zeros((32, 128), F32), hs, jnp.zeros((32, 128), F32)], 1)
 
     for side in range(2):
         flat = jnp.concatenate([col_in[side, s * G : (s + 1) * G] for s in range(SL)], 1)
-        back = dot(flip_r[...], flat)
+        back = dot(flip_r, flat)
         for s in range(SL):
             cols[side, 0, s] = col_in[side, s * G : (s + 1) * G].astype(F32)
             cols[side, 1, s] = back[:, 128 * s : 128 * s + 128]
@@ -333,19 +325,9 @@
         ecol.append(jnp.concatenate(pieces, 1))
         xright.append(got[0][:, 0:C])
         xleft.append(got[1][:, 0:C])
-    ecol = jnp.concatenate(ecol, 0)
+    rim_col[...] = jnp.concatenate(ecol, 0)
     xright = jnp.concatenate(xright, 0)
     xleft = jnp.concatenate(xleft, 0)
-    e3 = jnp.concatenate(
-        [pltpu.roll(ecol, 1, 0), ecol, pltpu.roll(ecol, R - 1, 0)], 1
-    ).astype(BF)
-    v2 = jnp.concatenate(
-        [v for a in range(3) for v in (tap(2 - a, 0), tap(a, 0), z32, z32)], 1
-    )
-    v3 = jnp.concatenate(
-        [v for a in range(3) for v in (z32, z32, tap(2 - a, 2), tap(a, 2))], 1
-    )
-    rim_col = dot_t(e3, jnp.concatenate([v2, v3], 0).astype(BF)).astype(BF).astype(F32)
     zc = jnp.zeros((R, C), F32)
     x1[:, 0:128] = jnp.concatenate([zc, zc, zc, xleft], 1).astype(BF)
     right = at(128 + 128 * 22, 128)
@@ -353,25 +335,25 @@
         x1[:, right].astype(F32) + jnp.concatenate([zc, zc, xright, zc], 1)
     ).astype(BF)
 
-    def move(n, c):
+    def move(n):
         left = x1[:, at(128 * n, 128)][:, 96:128]
         xp[:, at(128 * n, 128)] = jnp.concatenate(
             [left, x1[:, at(128 * n + 128, 128)][:, 0:96]], 1
         )
-        return c
-
-    lax.fori_loop(0, 24, move, 0)
+
+    for n in range(24):
+        move(n)
 
     gacc[...] = jnp.zeros_like(gacc)
 
-    def outer(m, c):
+    def outer(m):
         sv = jnp.concatenate([s3[2 - a, :, at(128 * m + 128, 128)] for a in range(3)], 1)
         gacc[...] += lax.dot_general(
             sv, xp[:, at(128 * m, 256)], (((0,), (0,)), ((), ())), preferred_element_type=F32
         )
-        return c
-
-    lax.fori_loop(0, 23, outer, 0)
+
+    for m in range(23):
+        outer(m)
     grad = gacc[...]
     for a in range(3):
         total = None
@@ -406,18 +388,44 @@
     bias_row = jnp.concatenate([bias[...]] * 8, 1)
 
     def forward(m, lanes):
-        xv = x1[:, at(256 * m + 128, 256)]
-        y = dot(down(xv), bands[0]) + dot(xv, bands[1])
-        y = y + dot(up(xv), bands[2]) + dot(beside(x1, m), wq) + bias_row
+        blk = at(256 * m + 128, 256)
+        y = dot(x3[0, :, blk], bands[0]) + dot(x3[1, :, blk], bands[1])
+        y = y + dot(x3[2, :, blk], bands[2]) + dot(beside(x1, m), wq[...]) + bias_row
         y = (y * wet[:, at(256 * m, 256)].astype(F32)).astype(BF)
         for s in range(SL):
             xs[s, :, at(256 * m, lanes)] = y[G * s : G * s + T, :lanes]
 
-    blocks(forward, first=False)
-    out_copies = []
-    for s in range(SL):
-        out_copies.append(pltpu.make_async_copy(xs.at[s], y_hbm.at[0, s], out_sem.at[0, s]))
-        out_copies[-1].start()
+    @pl.when(t >= 0)
+    def _():
+        for side, a in ((0, 2), (1, 0)):
+            total = None
+            for r in range(2):
+                rows = hs_ref[16 * side + 8 * r : 16 * side + 8 * r + 8]
+                lhs = jnp.concatenate(
+                    [rows[:, 256 * m : 256 * m + 512] for m in range(NB)], 0
+                ).astype(BF)
+                part_sum = dot_t(lhs, band(a, 16, 4, mirror=(r == 1)))
+                total = part_sum if total is None else total + part_sum
+            rim[side] = total.astype(BF).astype(F32)
+        ecol = rim_col[...]
+        z32 = jnp.zeros((C, C), F32)
+        e3 = jnp.concatenate(
+            [pltpu.roll(ecol, 1, 0), ecol, pltpu.roll(ecol, R - 1, 0)], 1
+        ).astype(BF)
+        v2 = jnp.concatenate(
+            [v for a in range(3) for v in (tap(2 - a, 0), tap(a, 0), z32, z32)], 1
+        )
+        v3 = jnp.concatenate(
+            [v for a in range(3) for v in (z32, z32, tap(2 - a, 2), tap(a, 2))], 1
+        )
+        rc = dot_t(e3, jnp.concatenate([v2, v3], 0).astype(BF)).astype(BF).astype(F32)
+        rim_col[...] = jnp.concatenate([rc, jnp.zeros((R, 64), F32)], 1)
+        for n in range(24):
+            xv = x1[:, at(128 * n + 128, 128)]
+            x3[0, :, at(128 * n + 128, 128)] = down(xv)
+            x3[2, :, at(128 * n + 128, 128)] = up(xv)
+        for m in range(5):
+            forward(m, 256)
 
     for copy in sends:
         copy.wait()
@@ -439,13 +447,24 @@
         sends.append(copy)
     got2[me] = total
 
+    @pl.when(t >= 0)
+    def _():
+        for m in range(5, NB):
+            forward(m, 256 if m < NB - 1 else LAST)
+
+    out_copies = []
+    for s in range(SL):
+        out_copies.append(pltpu.make_async_copy(xs.at[s], y_hbm.at[0, s], out_sem.at[0, s]))
+        out_copies[-1].start()
+
     row8 = lax.broadcasted_iota(jnp.int32, (8, 256), 0)
     z6 = jnp.zeros((R, 192), F32)
+    zc = jnp.zeros((R, C), F32)
 
     def backward(m, lanes):
         blk = at(256 * m + 128, 256)
         y = dot_t(s3[0, :, blk], bands[2]) + dot_t(s3[1, :, blk], bands[1])
-        y = y + dot_t(s3[2, :, blk], bands[0]) + dot_t(beside(s3.at[1], m), wqb)
+        y = y + dot_t(s3[2, :, blk], bands[0]) + dot_t(beside(s3.at[1], m), wqb[...])
         if isinstance(m, int) and m == 0:
             y = y + jnp.concatenate([rim_col[:, C : 2 * C], zc, z6], 1)
         if isinstance(m, int) and m == NB - 1:
@@ -462,9 +481,6 @@
         for s in range(SL):
             gs[s, :, at(256 * m, lanes)] = y[G * s : G * s + T, :lanes]
 
-    backward(0, 256)
-    lax.fori_loop(1, 6, lambda m, c: (backward(m, 256), c)[1], 0)
-
     for copy in sends:
         copy.wait()
     total = got2[0]
@@ -484,26 +500,67 @@
         copy.start()
         sends.append(copy)
 
-    lax.fori_loop(6, NB - 1, lambda m, c: (backward(m, 256), c)[1], 0)
-    backward(NB - 1, LAST)
+    @pl.when(t >= 0)
+    def _():
+        for m in range(NB):
+            backward(m, 256 if m < NB - 1 else LAST)
+
     for s in range(SL):
         out_copies.append(pltpu.make_async_copy(gs.at[s], gi_hbm.at[0, s], out_sem.at[1, s]))
         out_copies[-1].start()
 
     for copy in sends:
         copy.wait()
-    for a in range(3):
-        w_out[a] = full[C * a : C * a + C]
+    w_out[...] = jnp.concatenate([full[C * a : C * a + C, 0 : 3 * C] for a in range(3)], 1)
     b_out[...] = full[96:97, 0:C]
     for copy in out_copies:
         copy.wait()
 
 
+def settle_kernel(y_in, gi_in, w_in, b_in, y, gi, w, b, ys, gis, in_sem, out_sem):
+    pairs = ((y_in, ys, y), (gi_in, gis, gi))
+    loads = [
+        pltpu.make_async_copy(src.at[0, s], mid.at[s], in_sem.at[i, s])
+        for s in range(SL)
+        for i, (src, mid, dst) in enumerate(pairs)
+    ]
+    stores = [
+        pltpu.make_async_copy(mid.at[s], dst.at[0, s], out_sem.at[i, s])
+        for s in range(SL)
+        for i, (src, mid, dst) in enumerate(pairs)
+    ]
+    for load in loads:
+        load.start()
+    w[...] = w_in[...]
+    b[...] = b_in[...]
+    for load, store in zip(loads, stores):
+        load.wait()
+        store.start()
+    for store in stores:
+        store.wait()
+
+
+def settle(y, gi, w, b):
+    any_ = pl.BlockSpec(memory_space=pl.ANY)
+    vm = pl.BlockSpec(memory_space=pltpu.VMEM)
+    return pl.pallas_call(
+        settle_kernel,
+        in_specs=[any_, any_, vm, vm],
+        out_specs=[any_, any_, vm, vm],
+        out_shape=[jax.ShapeDtypeStruct(v.shape, v.dtype) for v in (y, gi, w, b)],
+        scratch_shapes=[
+            pltpu.VMEM((SL, T, W), BF),
+            pltpu.VMEM((SL, T, W), BF),
+            pltpu.SemaphoreType.DMA((2, SL)),
+            pltpu.SemaphoreType.DMA((2, SL)),
+        ],
+        compiler_params=pltpu.CompilerParams(vmem_limit_bytes=VMEM_LIMIT),
+    )(y, gi, w, b)
+
+
 def per_device(
     inputs, cotangent, conv_weight, out_bias, cell_area, land_mask, neighbours, reversal, wet_count
 ):
-    occupied = jnp.arange(SL, dtype=jnp.int32) < wet_count[0]
-    wa = jnp.where((land_mask != 0) & occupied[:, None], cell_area, 0.0).reshape(SL, T, T)
     n_face, n_tile, n_dp = (lax.axis_size(a) for a in ("face", "tile", "dp"))
     n_plane = n_face * n_dp
     scale = 1.0 / math.sqrt(n_dp * n_face * n_tile * SL * T * T)
@@ -514,18 +571,26 @@
     dma = pltpu.SemaphoreType.DMA
     outputs, input_grad, w_sum, b_sum = pl.pallas_call(
         functools.partial(device_kernel, (n_face, n_tile, n_dp, scale)),
-        in_specs=[sm, sm, any_, any_] + [vm] * 6,
+        in_specs=[sm, sm, any_, any_, sm] + [vm] * 4,
         out_specs=[any_, any_, vm, vm],
         out_shape=[
             tiles,
             tiles,
-            jax.ShapeDtypeStruct((3, C, 128), F32),
+            jax.ShapeDtypeStruct((C, 9 * C), F32),
             jax.ShapeDtypeStruct((1, C), F32),
         ],
         scratch_shapes=[
             pltpu.VMEM((SL, T, W), BF),
             pltpu.VMEM((SL, T, W), BF),
-            pltpu.VMEM((R, XW), BF),
+            pltpu.VMEM((256, WP), BF),
+            pltpu.VMEM((G, 8, 128), F32),
+            pltpu.VMEM((R, 256), BF),
+            pltpu.VMEM((3, 256, 256), BF),
+            pltpu.VMEM((256, 256), BF),
+            pltpu.VMEM((256, 256), BF),
+            pltpu.VMEM((R, 128), F32),
+            pltpu.VMEM((32, XW), F32),
+            pltpu.VMEM((3, R, XW), BF),
             pltpu.VMEM((3, R, XW), BF),
             pltpu.VMEM((R, WP), BF),
             pltpu.VMEM((R, WP), BF),
@@ -560,15 +625,14 @@
         reversal.T,
         inputs,
         cotangent,
-        wa,
-        jnp.asarray(spread_matrix()),
-        jnp.asarray(flip_lanes_matrix()),
-        jnp.asarray(flip_rows_matrix()),
+        wet_count,
+        cell_area,
+        land_mask,
         conv_weight.T,
         out_bias[None],
     )
-    weight_grad = w_sum[:, :, 0 : 3 * C].transpose(0, 2, 1).reshape(9 * C, C)
-    return outputs, input_grad, weight_grad, b_sum[0]
+    outputs, input_grad, w_sum, b_sum = settle(outputs, input_grad, w_sum, b_sum)
+    return outputs, input_grad, w_sum.T, b_sum[0]
 
 
 def solution(mesh):

time: 62.6 us -> 51.4 us (0.82)
  local copies, waits for them, and re-layouts: 9.03 us -> 0 us
  Pallas kernels: 50.9 us -> 49.7 us
  other arithmetic: 1.14 us -> 0 us
    pallas_call x1, Pallas kernels: 50.9 us -> 42.6 us  [per_device(): pl.pallas_call(functools.partial(device_kernel, (n_face, n_tile, n_dp, sc...]
    pallas_call x0 -> x1, Pallas kernels: none -> 7.18 us  [settle(): pl.pallas_call(settle_kernel, in_specs=[any_, any_, vm, vm], out_specs=[a...]
    unnamed x7 -> x0, local copies, waits for them, and re-layouts: 6.35 us -> none
    reshape x2 -> x0, local copies, waits for them, and re-layouts: 1.84 us -> none  [the longest x1 1.12 us: per_device(): jnp.where((land_mask != 0) & occupied[:, None], cell_area, 0.0)]
    select_n x1 -> x0, other arithmetic: 1.13 us -> none  [per_device(): jnp.where((land_mask != 0) & occupied[:, None], cell_area, 0.0)]
    transpose x2 -> x0, local copies, waits for them, and re-layouts: 0.84 us -> none  [per_device(): weight_grad = w_sum[:, :, 0:3 * C].transpose(0, 2, 1).reshape(9 * C, C)]
where the time goes in v3:
time: 51.4 us; the launch traced here: 51.2 us
  Pallas kernels  49.7 us (97%)
  between operations  1.47 us (3%)
    pallas_call x1, Pallas kernels, per_device(): pl.pallas_call(functools.partial(device_kernel, (n_face, n_tile, n_dp, sc...  42.6 us
    pallas_call x1, Pallas kernels, settle(): pl.pallas_call(settle_kernel, in_specs=[any_, any_, vm, vm], out_specs=[a...  7.18 us

profile of v3, /device:TPU:1, one launch (start us, length us, event | category | flops | bytes accessed | tf_op | source)
XLA Modules:
  0.0 51.2 jit_solution(17989759424370275921)
XLA Ops:
  1.3 42.6 %shard_map.120 = (bf16[1,6,90,2880]{3,2,1,0:T(8,128)(2,1)}, bf16[1,6,90,2880]{3,2,1,0:T(8,128)(2,1)}, f32[32,288]{1,0:T(8,128)}, f32[1,32]{1,0:T(1,128)}) custom-call(s32[4,6]{1,0:T(4,128)} %bitcast.7, s32[4,6]{1,0:T(4,128)} %bitcast.8, bf16[1,6,90,2880]{3,2,1,0:T(8,128)(2,1)} %x_hbm.1, bf16[1,6,90,2880]{3,2,1,0:T(8,128)(2,1)} %g_hbm.1, s32[1]{0:T(128)S(6)} %copy.13.count, ...), custom_call_target="tpu_custom_call" | custom-call | tf_op jit(solution)/shard_map/pallas_call | solution.py:572
  43.9 7.2 %shard_map.121 = (bf16[1,6,90,2880]{3,2,1,0:T(8,128)(2,1)}, bf16[1,6,90,2880]{3,2,1,0:T(8,128)(2,1)}, f32[32,288]{1,0:T(8,128)}, f32[1,32]{1,0:T(1,128)}) custom-call(bf16[1,6,90,2880]{3,2,1,0:T(8,128)(2,1)} %get-tuple-element.12.y_in, bf16[1,6,90,2880]{3,2,1,0:T(8,128)(2,1)} %get-tuple-element.13.gi_in, f32[32,288]{1,0:T(8,128)} %get-tuple-element.14.w_in, ...), custom_call_target="tpu_custom_call" | custom-call | tf_op jit(solution)/shard_map/pallas_call | solution.py:546

commit v4 on v3

--- a/solution.py
+++ b/solution.py
@@ -138,42 +138,39 @@
             out = jnp.where(which == c, jnp.concatenate([wide] * 8, 0), out)
         return out.astype(BF)
 
+    slot_i = lax.broadcasted_iota(jnp.int32, (SL, T * T), 0)
+    flat = jnp.where((mask_in[...] != 0) & (slot_i < count[0]), area_in[...], 0.0)
+    flat = jnp.concatenate([flat, jnp.zeros((2, T * T), F32)], 0)
+    for i in range(T):
+        by_row[i] = jnp.concatenate([flat[:, T * i : T * i + T], jnp.zeros((8, 128 - T), F32)], 1)
+    by_row[T:G] = jnp.zeros((G - T, 8, 128), F32)
+    wa = [by_row[:, s, :] for s in range(SL)]
+    hi, lo = split_hi_lo(jnp.concatenate(wa, 0))
+    area_ref[...] = jnp.concatenate([hi, lo], 1)
+
+    for m in range(NB):
+        r_i = lax.broadcasted_iota(jnp.int32, (256, 256), 0)
+        l_i = lax.broadcasted_iota(jnp.int32, (256, 256), 1)
+        hit = (r_i & 127) == (l_i >> 5) + 8 * m
+        spread[:, 256 * m : 256 * m + 256] = jnp.where(hit & ((r_i & 127) < T), 1.0, 0.0).astype(BF)
+
+    for a in range(3):
+        bands[a] = band(a, 8, 0)
+    z32 = jnp.zeros((C, C), F32)
+    z64 = jnp.zeros((C, 192), F32)
+    wq_rows = []
+    for a in range(3):
+        wq_rows.append(jnp.concatenate([tap(a, 0), z32, z64], 1))
+        wq_rows.append(jnp.concatenate([z64, z32, tap(a, 2)], 1))
+    wq[...] = jnp.concatenate(wq_rows + [jnp.zeros((64, 256), F32)], 0).astype(BF)
+    gl = jnp.concatenate([v for a in range(3) for v in (tap(2 - a, 2), z32)] + [z32, z32], 1)
+    gr = jnp.concatenate([v for a in range(3) for v in (z32, tap(2 - a, 0))] + [z32, z32], 1)
+    wqb[...] = jnp.concatenate([gl, jnp.zeros((192, 256), F32), gr], 0).astype(BF)
+
     @pl.when(t >= 0)
     def _():
-        slot_i = lax.broadcasted_iota(jnp.int32, (SL, T * T), 0)
-        flat = jnp.where((mask_in[...] != 0) & (slot_i < count[0]), area_in[...], 0.0)
-        flat = jnp.concatenate([flat, jnp.zeros((2, T * T), F32)], 0)
-        for i in range(T):
-            by_row[i] = jnp.concatenate([flat[:, T * i : T * i + T], jnp.zeros((8, 128 - T), F32)], 1)
-        by_row[T:G] = jnp.zeros((G - T, 8, 128), F32)
-        wa = [by_row[:, s, :] for s in range(SL)]
-        hi, lo = split_hi_lo(jnp.concatenate(wa, 0))
-        area_ref[...] = jnp.concatenate([hi, lo], 1)
-
-        for m in range(NB):
-            r_i = lax.broadcasted_iota(jnp.int32, (256, 256), 0)
-            l_i = lax.broadcasted_iota(jnp.int32, (256, 256), 1)
-            hit = (r_i & 127) == (l_i >> 5) + 8 * m
-            spread[:, 256 * m : 256 * m + 256] = jnp.where(hit & ((r_i & 127) < T), 1.0, 0.0).astype(BF)
-
-        for a in range(3):
-            bands[a] = band(a, 8, 0)
-        z32 = jnp.zeros((C, C), F32)
-        z64 = jnp.zeros((C, 192), F32)
-        wq_rows = []
-        for a in range(3):
-            wq_rows.append(jnp.concatenate([tap(a, 0), z32, z64], 1))
-            wq_rows.append(jnp.concatenate([z64, z32, tap(a, 2)], 1))
-        wq[...] = jnp.concatenate(wq_rows + [jnp.zeros((64, 256), F32)], 0).astype(BF)
-        gl = jnp.concatenate([v for a in range(3) for v in (tap(2 - a, 2), z32)] + [z32, z32], 1)
-        gr = jnp.concatenate([v for a in range(3) for v in (z32, tap(2 - a, 0))] + [z32, z32], 1)
-        wqb[...] = jnp.concatenate([gl, jnp.zeros((192, 256), F32), gr], 0).astype(BF)
-
-    for copy in copies:
-        copy.wait()
-
-    @pl.when(t >= 0)
-    def _():
+        for copy in copies:
+            copy.wait()
         wa = [by_row[:, s, :] for s in range(SL)]
         for side, row in ((0, 0), (1, T - 1)):
             lhs = [by_row[row, s : s + 1, :] for s in range(SL)] + [jnp.zeros((2, 128), F32)]

time: 51.4 us -> 51.4 us (level)
  no operation moved by 1% of the time
where the time goes in v4:
time: 51.4 us; the launch traced here: 51.2 us
  Pallas kernels  49.7 us (97%)
  between operations  1.47 us (3%)
    pallas_call x1, Pallas kernels, per_device(): pl.pallas_call(functools.partial(device_kernel, (n_face, n_tile, n_dp, sc...  42.6 us
    pallas_call x1, Pallas kernels, settle(): pl.pallas_call(settle_kernel, in_specs=[any_, any_, vm, vm], out_specs=[a...  7.18 us

profile of v4, /device:TPU:1, one launch (start us, length us, event | category | flops | bytes accessed | tf_op | source)
XLA Modules:
  0.0 51.2 jit_solution(8661549751546880224)
XLA Ops:
  1.3 42.6 %shard_map.120 = (bf16[1,6,90,2880]{3,2,1,0:T(8,128)(2,1)}, bf16[1,6,90,2880]{3,2,1,0:T(8,128)(2,1)}, f32[32,288]{1,0:T(8,128)}, f32[1,32]{1,0:T(1,128)}) custom-call(s32[4,6]{1,0:T(4,128)} %bitcast.7, s32[4,6]{1,0:T(4,128)} %bitcast.8, bf16[1,6,90,2880]{3,2,1,0:T(8,128)(2,1)} %x_hbm.1, bf16[1,6,90,2880]{3,2,1,0:T(8,128)(2,1)} %g_hbm.1, s32[1]{0:T(128)S(6)} %copy.13.count, ...), custom_call_target="tpu_custom_call" | custom-call | tf_op jit(solution)/shard_map/pallas_call | solution.py:569
  43.8 7.2 %shard_map.121 = (bf16[1,6,90,2880]{3,2,1,0:T(8,128)(2,1)}, bf16[1,6,90,2880]{3,2,1,0:T(8,128)(2,1)}, f32[32,288]{1,0:T(8,128)}, f32[1,32]{1,0:T(1,128)}) custom-call(bf16[1,6,90,2880]{3,2,1,0:T(8,128)(2,1)} %get-tuple-element.12.y_in, bf16[1,6,90,2880]{3,2,1,0:T(8,128)(2,1)} %get-tuple-element.13.gi_in, f32[32,288]{1,0:T(8,128)} %get-tuple-element.14.w_in, ...), custom_call_target="tpu_custom_call" | custom-call | tf_op jit(solution)/shard_map/pallas_call | solution.py:543
